TPU v7x, 256 devices: a whole 4x4x8 slice. The times are simulated.
256 devices in a mesh: blk: 16 (over x, y_hi, core), rep: 16 (over y_lo, z).
Axes of the slice: x: 4, y: 4 (y_hi: 2, y_lo: 2; y = y_hi * 2 + y_lo), z: 8, core: 2. Of those that a mesh axis runs over, the one named last changes fastest.
Arguments:
- tokens: bfloat16 [32768, 2048], P(('blk', 'rep')), may hold values from -24 to 24
- grad_out: bfloat16 [32768, 2048], P(('blk', 'rep')), may hold values from -1 to 1
- expert_ids: int32 [32768, 2], P(('blk', 'rep')), may hold values from 0 to 15, all different within a row; in each aligned block of 128 rows (0 to 127, 128 to 255, ...) at most 32 rows name the same one
- gates: bfloat16 [32768, 2], P(('blk', 'rep')), may hold values from 0.099609375 to 1
- gate_up_weight: bfloat16 [16, 2048, 1536], P('blk'), may hold values from -0.125 to 0.125
- down_weight: bfloat16 [16, 2048, 768], P('blk'), may hold values from -0.21875 to 0.21875
Outputs:
- grad_tokens: bfloat16 [32768, 2048], P(('blk', 'rep'))
- grad_gates: bfloat16 [32768, 2], P(('blk', 'rep'))
- grad_gate_up: float32 [16, 2048, 1536], P('blk', 'rep')
- grad_down: float32 [16, 2048, 768], P('blk', 'rep')
Inputs may be any that keep to these rules, and one draw needn't show every extreme that they name: `expert_ids`: the 2 experts of a token differ. Among the rows of one device, no expert is named more than 32 times.
All inputs are finite; a program needn't handle non-finite values.
Results may differ from a plain program's by a relative error of at most 0.0065.
Values may be sent and summed in bfloat16 or wider, within the bound.
No kernel may reach another device: no remote copies, remote signals or barrier semaphores. Data moves between devices by JAX's collectives and lax.ppermute only.
A program may use at most 192 MiB of HBM per device.

v0:
```python
import jax
import jax.numpy as jnp
from jax import lax
from jax.sharding import PartitionSpec as P


def expert_rows(row_inputs, row_grads, row_gates, gate_matrix, down_matrix):
    projected = jnp.dot(row_inputs, gate_matrix, preferred_element_type=jnp.float32)
    hidden_width = down_matrix.shape[1]
    gate_part = projected[:, :hidden_width]
    up_part = projected[:, hidden_width:]
    sigmoid_gate = jax.nn.sigmoid(gate_part)
    silu_gate = gate_part * sigmoid_gate
    hidden = (silu_gate * up_part).astype(jnp.bfloat16)
    expert_out = lax.dot_general(
        hidden, down_matrix, (((1,), (1,)), ((), ())), preferred_element_type=jnp.float32
    )
    gate_grad = jnp.sum(row_grads.astype(jnp.float32) * expert_out, axis=1).astype(jnp.bfloat16)
    scaled = (row_gates.astype(jnp.float32)[:, None] * row_grads.astype(jnp.float32)).astype(
        jnp.bfloat16
    )
    grad_hidden = jnp.dot(scaled, down_matrix, preferred_element_type=jnp.float32)
    grad_gate_part = grad_hidden * up_part * sigmoid_gate * (1.0 + gate_part * (1.0 - sigmoid_gate))
    grad_up_part = grad_hidden * silu_gate
    grad_pre = jnp.concatenate([grad_gate_part, grad_up_part], axis=1).astype(jnp.bfloat16)
    row_grad = lax.dot_general(
        grad_pre, gate_matrix, (((1,), (1,)), ((), ())), preferred_element_type=jnp.float32
    ).astype(jnp.bfloat16)
    return (hidden, scaled, grad_pre, row_grad, gate_grad)


def outer_sum(left_rows, right_rows):
    return lax.dot_general(
        left_rows, right_rows, (((0,), (0,)), ((), ())), preferred_element_type=jnp.float32
    )


def shards(tokens, grad_out, expert_ids, gates, gate_up_weight, down_weight):
    token_count, top_count = expert_ids.shape
    model_width = tokens.shape[1]
    experts = lax.axis_size("blk")
    capacity = 2 * token_count * top_count // experts
    slot_count = experts * capacity
    row_count = token_count * top_count
    gate_matrix = gate_up_weight[0]
    down_matrix = down_weight[0]
    flat_ids = expert_ids.reshape(row_count)
    onehot = (flat_ids[:, None] == jnp.arange(experts, dtype=jnp.int32)[None, :]).astype(jnp.int32)
    before = jnp.cumsum(onehot, axis=0) - onehot
    target = flat_ids * capacity + jnp.sum(before * onehot, axis=1)
    matches = target[None, :] == jnp.arange(slot_count, dtype=jnp.int32)[:, None]
    filled = jnp.any(matches, axis=1)
    source = jnp.sum(jnp.where(matches, jnp.arange(row_count, dtype=jnp.int32)[None, :], 0), axis=1)
    token_of = source // top_count
    send_rows = jnp.where(filled[:, None], tokens[token_of], jnp.zeros((), tokens.dtype)).reshape(
        experts, capacity, model_width
    )
    send_grads = jnp.where(
        filled[:, None], grad_out[token_of], jnp.zeros((), grad_out.dtype)
    ).reshape(experts, capacity, model_width)
    send_gates = jnp.where(
        filled, gates.reshape(row_count)[source], jnp.zeros((), gates.dtype)
    ).reshape(experts, capacity)
    home_rows, home_grads, home_gates = (
        lax.all_to_all(send_rows, "blk", split_axis=0, concat_axis=0, tiled=True),
        lax.all_to_all(send_grads, "blk", split_axis=0, concat_axis=0, tiled=True),
        lax.all_to_all(send_gates, "blk", split_axis=0, concat_axis=0, tiled=True),
    )
    home_rows = home_rows.reshape(slot_count, model_width)
    home_grads = home_grads.reshape(slot_count, model_width)
    home_gates = home_gates.reshape(slot_count)
    hidden, scaled, grad_pre, row_grad, gate_grad = expert_rows(
        home_rows, home_grads, home_gates, gate_matrix, down_matrix
    )
    down_total = lax.psum_scatter(outer_sum(scaled, hidden), "rep", scatter_dimension=0, tiled=True)
    gate_up_total = lax.psum_scatter(
        outer_sum(home_rows, grad_pre), "rep", scatter_dimension=0, tiled=True
    )
    back_grads, back_gates = (
        lax.all_to_all(
            row_grad.reshape(experts, capacity, model_width),
            "blk",
            split_axis=0,
            concat_axis=0,
            tiled=True,
        ),
        lax.all_to_all(
            gate_grad.reshape(experts, capacity), "blk", split_axis=0, concat_axis=0, tiled=True
        ),
    )
    per_row = back_grads.reshape(slot_count, model_width)[target]
    grad_tokens = jnp.sum(
        per_row.reshape(token_count, top_count, model_width).astype(jnp.float32), axis=1
    ).astype(jnp.bfloat16)
    grad_gates = back_gates.reshape(slot_count)[target].reshape(token_count, top_count)
    return (grad_tokens, grad_gates, gate_up_total[None], down_total[None])


def solution(mesh):
    in_specs = (
        P(("blk", "rep"), None),
        P(("blk", "rep"), None),
        P(("blk", "rep"), None),
        P(("blk", "rep"), None),
        P("blk", None, None),
        P("blk", None, None),
    )
    out_specs = (
        P(("blk", "rep"), None),
        P(("blk", "rep"), None),
        P("blk", "rep", None),
        P("blk", "rep", None),
    )
    return jax.shard_map(shards, mesh=mesh, in_specs=in_specs, out_specs=out_specs, check_vma=False)
```

profile of v0, /device:TPU:1, one launch (start us, length us, event | category | flops | bytes accessed | tf_op | source)
XLA Modules:
  0.0 376.4 jit_solution(4137685434093486461)
XLA Ops:
  7.2 0.0 copy-start
  7.2 0.9 copy.31
  8.1 0.1 reshape.228
  8.3 0.1 eq.39
  8.4 0.6 reduce-window.6
  9.0 0.2 slice_reduce_fusion
  9.2 0.1 fusion.18
  9.3 0.2 fusion.15
  9.5 0.2 select_reduce_fusion
  9.7 0.8 copy.34
  10.4 0.1 reshape.230
  10.6 3.4 gather_fusion
  14.0 0.7 select_n.81
  14.7 8.4 %all-to-all-start = ((bf16[16,1,32]{2,1,0:T(2,128)(2,1)}), bf16[16,1,32]{2,1,0:T(2,128)(2,1)S(1)}, u32[]{:S(2)}, u32[]{:S(2)}) async-start(bf16[16,1,32]{2,1,0:T(2,128)(2,1)} %select_n.81), calls=%async_computation | async-start | bytes 16384 | tf_op jit(solution)/shard_map/all_to_all | solution.py:67
  23.1 0.1 broadcast_in_dim.55
  23.2 6.4 %gather_fusion.2 = bf16[512,2048]{1,0:T(8,128)(2,1)} fusion(bf16[128,2048]{1,0:T(8,128)(2,1)} %param.6, s32[1024]{0:T(1024)S(1)} %pad_clamp_fusion.1), kind=kCustom, calls=%fused_computation.2 | custom fusion | bytes 4196352 | tf_op jit(solution)/shard_map/gather | solution.py:55
  29.6 6.4 %gather_fusion.1 = bf16[512,2048]{1,0:T(8,128)(2,1)} fusion(bf16[128,2048]{1,0:T(8,128)(2,1)} %param.7, s32[1024]{0:T(1024)S(1)} %pad_clamp_fusion.1), kind=kCustom, calls=%fused_computation.1 | custom fusion | bytes 4196352 | tf_op jit(solution)/shard_map/gather | solution.py:59
  36.0 4.6 %broadcast_select_fusion = (bf16[16,32,2048]{2,1,0:T(8,128)(2,1)}, bf16[16,32,2048]{2,1,0:T(8,128)(2,1)}) fusion(bf16[16,32,2048]{2,1,0:T(8,128)(2,1)} %bitcast.60, pred[16,32]{1,0:T(8,128)(4,1)S(1)} %broadcast_in_dim.55, bf16[16,32,2048]{2,1,0:T(8,128)(2,1)} %bitcast.61), kind=kLoop, calls=%fused_computation.19 | loop fusion | flops 2097152 | bytes 8389120 | tf_op jit(solution)/shard_map/jit(_where)/select_n | solution.py:55
  40.6 0.0 all-to-all-done
  40.6 35.3 %all_to_all.27 = bf16[16,32,2048]{2,1,0:T(8,128)(2,1)} all-to-all(bf16[16,32,2048]{2,1,0:T(8,128)(2,1)} %get-tuple-element.23), channel_id=1, replica_groups=mesh['blk'=16,'rep'=16] {'blk'}, dimensions={0} | all-to-all | bytes 4194304 | tf_op jit(solution)/shard_map/all_to_all | solution.py:65
  75.9 5.5 %all-to-all-start.1 = ((bf16[16,32,2048]{2,1,0:T(8,128)(2,1)}), bf16[16,32,2048]{2,1,0:T(8,128)(2,1)}, u32[]{:S(2)}, u32[]{:S(2)}) async-start(bf16[16,32,2048]{2,1,0:T(8,128)(2,1)} %get-tuple-element.24), calls=%async_computation.1 | async-start | bytes 4194304 | tf_op jit(solution)/shard_map/all_to_all | solution.py:66
  81.4 0.2 reduce-scatter.5.cloned.1.call-start
  81.7 0.1 reshape.239
  81.7 8.5 %fusion.2 = f32[512,1536]{1,0:T(8,128)} fusion(bf16[512,2048]{1,0:T(8,128)(2,1)} %bitcast.62, bf16[1,2048,1536]{2,1,0:T(8,128)(2,1)} %param.10), kind=kOutput, calls=%fused_computation.7 | convolution fusion | flops 3221225472 | bytes 11534336 | tf_op jit(solution)/shard_map/dot_general | solution.py:8
  90.3 19.8 %all-to-all-done.1 = bf16[16,32,2048]{2,1,0:T(8,128)(2,1)} async-done(((bf16[16,32,2048]{2,1,0:T(8,128)(2,1)}), bf16[16,32,2048]{2,1,0:T(8,128)(2,1)}, u32[]{:S(2)}, u32[]{:S(2)}) %all-to-all-start.1) | async-done | bytes 2097184 | tf_op jit(solution)/shard_map/all_to_all | solution.py:66
  110.0 0.0 copy-start.3
  110.0 2.1 fusion.4
  112.2 0.0 copy-done
  112.2 0.4 copy-done.3
  112.6 3.4 multiply_convert_fusion.2
  116.0 0.0 copy-start.1
  116.0 2.3 fusion.6
  118.2 0.0 copy-done.1
  118.3 4.5 %fusion.22 = f32[2048,768]{1,0:T(8,128)} fusion(bf16[512,2048]{1,0:T(8,128)(2,1)S(1)} %fusion.6, bf16[512,768]{1,0:T(8,128)(2,1)S(1)} %get-tuple-element.22), kind=kOutput, calls=%fused_computation.56 | convolution fusion | flops 1610612736 | bytes 9175040 | tf_op jit(solution)/shard_map/dot_general | solution.py:33
  122.7 0.0 reduce-scatter.5.cloned.1.call-update
  122.8 0.0 reduce-scatter.3.cloned.1.call-start
  122.8 10.0 %fusion.14 = f32[2048,1536]{1,0:T(8,128)} fusion(bf16[512,2048]{1,0:T(8,128)(2,1)} %bitcast.63, bf16[512,768]{1,0:T(8,128)(2,1)} %get-tuple-element.21, bf16[512,768]{1,0:T(8,128)(2,1)} %get-tuple-element.20), kind=kOutput, calls=%fused_computation.27 | convolution fusion | flops 3224371200 | bytes 16252928 | tf_op jit(solution)/shard_map/dot_general | solution.py:33
  132.8 0.0 reduce-scatter.3.cloned.1.call-update
  132.9 3.8 fusion.5
  136.6 0.7 convert_element_type.83
  137.3 5.5 %all-to-all-start.4 = ((bf16[16,1,32]{2,1,0:T(2,128)(2,1)}), bf16[16,1,32]{2,1,0:T(2,128)(2,1)S(1)}, u32[]{:S(2)}, u32[]{:S(2)}) async-start(bf16[16,1,32]{2,1,0:T(2,128)(2,1)} %convert_element_type.83), calls=%async_computation.4 | async-start | bytes 16384 | tf_op jit(solution)/shard_map/all_to_all | solution.py:87
  142.8 8.1 %fusion.10 = bf16[512,2048]{1,0:T(8,128)(2,1)} fusion(bf16[1,2048,1536]{2,1,0:T(8,128)(2,1)} %param.10, bf16[512,768]{1,0:T(8,128)(2,1)} %get-tuple-element.21, bf16[512,768]{1,0:T(8,128)(2,1)} %get-tuple-element.20), kind=kOutput, calls=%fused_computation.18 | convolution fusion | flops 3225419776 | bytes 9961472 | tf_op jit(solution)/shard_map/dot_general | solution.py:26
  150.9 0.0 all-to-all-done.4
  150.9 0.0 copy-start.2
  150.9 7.4 %all-to-all-start.3 = ((bf16[16,32,2048]{2,1,0:T(8,128)(2,1)}), bf16[16,32,2048]{2,1,0:T(8,128)(2,1)}, u32[]{:S(2)}, u32[]{:S(2)}) async-start(bf16[16,32,2048]{2,1,0:T(8,128)(2,1)} %bitcast.64), calls=%async_computation.3 | async-start | bytes 4194304 | tf_op jit(solution)/shard_map/all_to_all | solution.py:80
  158.3 0.0 copy-done.2
  158.3 0.1 copy.36
  158.4 0.1 mul.77
  158.6 0.1 reshape.235
  158.7 1.9 gather_fusion.4
  160.7 0.2 reshape.236
  160.8 0.6 copy.38
  161.4 66.5 %all-to-all-done.3 = bf16[16,32,2048]{2,1,0:T(8,128)(2,1)} async-done(((bf16[16,32,2048]{2,1,0:T(8,128)(2,1)}), bf16[16,32,2048]{2,1,0:T(8,128)(2,1)}, u32[]{:S(2)}, u32[]{:S(2)}) %all-to-all-start.3) | async-done | bytes 2097184 | tf_op jit(solution)/shard_map/all_to_all | solution.py:80
  227.9 5.2 %gather_fusion.3 = bf16[256,2048]{1,0:T(8,128)(2,1)} fusion(bf16[512,2048]{1,0:T(8,128)(2,1)} %bitcast.12, s32[1024]{0:T(1024)S(1)} %pad_clamp_fusion), kind=kCustom, calls=%fused_computation.3 | custom fusion | bytes 2098176 | tf_op jit(solution)/shard_map/gather | solution.py:91
  233.1 2.5 reshape.234
  235.7 4.6 %reduce_sum.47 = bf16[128,2048]{1,0:T(8,128)(2,1)} reduce(bf16[128,2,2048]{2,1,0:T(2,128)(2,1)} %reshape.234, bf16[]{:T(256)} %constant.31.clone.1), dimensions={1}, to_apply=%region_5.6 | reduce | flops 262144 | bytes 1572866 | tf_op jit(solution)/shard_map/reduce_sum | solution.py:92
  240.3 0.0 reduce-scatter.5.cloned.1.call-done
  240.3 129.3 %reduce-scatter.3.cloned.1.call-done = f32[128,1536]{1,0:T(8,128)} async-done(((f32[2048,1536]{1,0:T(8,128)}), f32[128,1536]{1,0:T(8,128)}) %reduce-scatter.3.cloned.1.call-update) | async-done | bytes 786448 | tf_op jit(solution)/shard_map/reduce_scatter | solution.py:76
  (14 shorter events, 0.2 us)
Async XLA Ops:
  7.2 105.0 %copy-start = (bf16[1,2048,768]{2,1,0:T(8,128)(2,1)S(1)}, bf16[1,2048,768]{2,1,0:T(8,128)(2,1)}, u32[]{:S(2)}) copy-start(bf16[1,2048,768]{2,1,0:T(8,128)(2,1)} %param.11) | copy-start | bytes 9437188
  14.7 25.9 %all-to-all-start = ((bf16[16,1,32]{2,1,0:T(2,128)(2,1)}), bf16[16,1,32]{2,1,0:T(2,128)(2,1)S(1)}, u32[]{:S(2)}, u32[]{:S(2)}) async-start(bf16[16,1,32]{2,1,0:T(2,128)(2,1)} %select_n.81), calls=%async_computation | async-start | bytes 16384 | tf_op jit(solution)/shard_map/all_to_all | solution.py:67
  75.9 34.1 %all-to-all-start.1 = ((bf16[16,32,2048]{2,1,0:T(8,128)(2,1)}), bf16[16,32,2048]{2,1,0:T(8,128)(2,1)}, u32[]{:S(2)}, u32[]{:S(2)}) async-start(bf16[16,32,2048]{2,1,0:T(8,128)(2,1)} %get-tuple-element.24), calls=%async_computation.1 | async-start | bytes 4194304 | tf_op jit(solution)/shard_map/all_to_all | solution.py:66
  81.4 158.9 %reduce-scatter.5.cloned.1.call-start = ((), (), s32[]{:S(2)}) async-start(), calls=%async_computation.8 | async-start | bytes 6684672 | tf_op jit(solution)/shard_map/reduce_scatter | solution.py:75
  110.0 2.5 copy-start.3
  116.0 2.3 copy-start.1
  122.8 246.8 %reduce-scatter.3.cloned.1.call-start = ((), (), s32[]{:S(2)}) async-start(), calls=%async_computation.7 | async-start | bytes 13369344 | tf_op jit(solution)/shard_map/reduce_scatter | solution.py:76
  137.3 13.6 %all-to-all-start.4 = ((bf16[16,1,32]{2,1,0:T(2,128)(2,1)}), bf16[16,1,32]{2,1,0:T(2,128)(2,1)S(1)}, u32[]{:S(2)}, u32[]{:S(2)}) async-start(bf16[16,1,32]{2,1,0:T(2,128)(2,1)} %convert_element_type.83), calls=%async_computation.4 | async-start | bytes 16384 | tf_op jit(solution)/shard_map/all_to_all | solution.py:87
  150.9 7.4 %copy-start.2 = (s32[128,2]{0,1:T(2,128)S(1)}, s32[128,2]{0,1:T(2,128)}, u32[]{:S(2)}) copy-start(s32[128,2]{0,1:T(2,128)} %param.8) | copy-start | bytes 3076
  150.9 77.0 %all-to-all-start.3 = ((bf16[16,32,2048]{2,1,0:T(8,128)(2,1)}), bf16[16,32,2048]{2,1,0:T(8,128)(2,1)}, u32[]{:S(2)}, u32[]{:S(2)}) async-start(bf16[16,32,2048]{2,1,0:T(8,128)(2,1)} %bitcast.64), calls=%async_computation.3 | async-start | bytes 4194304 | tf_op jit(solution)/shard_map/all_to_all | solution.py:80
Sparse Core Ops, SparseCore 0:
  122.9 97.0 reduce-scatter.4
  223.1 146.3 reduce-scatter.2
where the time goes:
time: 377 us; the launch traced here: 376 us
  waiting for transfers between devices  216 us (57%)
  matrix products  38.3 us (10%)
  blocking collectives  35.3 us (9%)
  local copies, waits for them, and re-layouts  31.2 us (8%)
  starting transfers between devices  27 us (7%)
  other arithmetic  14.7 us (4%)
  between operations  14.2 us (4%)
    reduce_scatter x1, waiting for transfers between devices, shards(): lax.psum_scatter(outer_sum(home_rows, grad_pre), 'rep', scatter_dimension...  129 us
    all_to_all x1, waiting for transfers between devices, shards(): lax.all_to_all(row_grad.reshape(experts, capacity, model_width), 'blk', s...  66.5 us
    all_to_all x1, blocking collectives, shards(): lax.all_to_all(send_rows, 'blk', split_axis=0, concat_axis=0, tiled=True)  35.3 us
    all_to_all x1, waiting for transfers between devices, shards(): lax.all_to_all(send_grads, 'blk', split_axis=0, concat_axis=0, tiled=True)  19.8 us
    dot_general x2, matrix products, outer_sum(): lax.dot_general(left_rows, right_rows, (((0,), (0,)), ((), ())), preferre...  14.5 us
    dot_general x1, matrix products, expert_rows(): jnp.dot(row_inputs, gate_matrix, preferred_element_type=jnp.float32)  8.5 us
    all_to_all x1, starting transfers between devices, shards(): lax.all_to_all(send_gates, 'blk', split_axis=0, concat_axis=0, tiled=True)  8.45 us
    dot_general x1, matrix products, expert_rows(): lax.dot_general(grad_pre, gate_matrix, (((1,), (1,)), ((), ())), preferre...  8.11 us
  transfers between devices with their start and end apart: 6, of which 3 were waited for; matrix products, arithmetic and copies ran while one was open for 17% of the time, Pallas kernels for 0%

commit v1 on v0

v1 whole, which is shorter than its diff:
```python
import functools

import jax
import jax.numpy as jnp
from jax import lax
from jax.experimental import pallas as pl
from jax.experimental.pallas import tpu as pltpu
from jax.sharding import PartitionSpec as P

BF16 = jnp.bfloat16
F32 = jnp.float32
LANES = 128
MIB = 1024 * 1024


def dot(left, right, left_dim=1, right_dim=0):
    return lax.dot_general(
        left, right, (((left_dim,), (right_dim,)), ((), ())), preferred_element_type=F32
    )


def dispatch_kernel(ids_ref, gates_ref, tokens_ref, grads_ref, send_ref, target_ref, *, experts):
    count = ids_ref.shape[1]
    slots = send_ref.shape[0]
    width = tokens_ref.shape[1]
    capacity = slots // experts
    first, second = ids_ref[0:1, :], ids_ref[1:2, :]
    expert = lax.broadcasted_iota(jnp.int32, (experts, count), 0)
    first_hot, second_hot = first == expert, second == expert
    earlier = (
        lax.broadcasted_iota(jnp.int32, (count, count), 0)
        < lax.broadcasted_iota(jnp.int32, (count, count), 1)
    ).astype(F32).astype(BF16)
    first_count, second_count = first_hot.astype(F32), second_hot.astype(F32)
    first_before = dot(first_count.astype(BF16), earlier)
    second_before = dot(second_count.astype(BF16), earlier) + jnp.sum(
        first_count, axis=1, keepdims=True
    )
    first_slot = first * capacity + jnp.sum(
        first_count * first_before, axis=0, keepdims=True
    ).astype(jnp.int32)
    second_slot = second * capacity + jnp.sum(
        second_count * second_before, axis=0, keepdims=True
    ).astype(jnp.int32)
    target_ref[0:1, :] = first_slot
    target_ref[1:2, :] = second_slot
    slot = lax.broadcasted_iota(jnp.int32, (slots, count), 0)
    gates = gates_ref[...].astype(F32)
    from_first, from_second = slot == first_slot, slot == second_slot
    pick = jnp.where(from_first | from_second, 1.0, 0.0).astype(BF16)
    scale = jnp.where(
        from_first, gates[0:1, :], jnp.where(from_second, gates[1:2, :], 0.0)
    ).astype(BF16)
    step = 512
    for at in range(0, width, step):
        send_ref[:, at : at + step] = dot(pick, tokens_ref[:, at : at + step]).astype(BF16)
        send_ref[:, width + at : width + at + step] = dot(
            scale, grads_ref[:, at : at + step]
        ).astype(BF16)


def rows_kernel(rows_ref, gate_ref, up_ref, down_ref, hidden_ref, pre_gate_ref, pre_up_ref, gate_sum_ref):
    width = down_ref.shape[0]
    inputs, scaled = rows_ref[:, :width], rows_ref[:, width:]
    gate_part = dot(inputs, gate_ref[...])
    up_part = dot(inputs, up_ref[...])
    grad_hidden = dot(scaled, down_ref[...])
    sigmoid_gate = jax.nn.sigmoid(gate_part)
    silu_gate = gate_part * sigmoid_gate
    hidden = silu_gate * up_part
    hidden_ref[...] = hidden.astype(BF16)
    pre_gate_ref[...] = (
        grad_hidden * up_part * sigmoid_gate * (1.0 + gate_part * (1.0 - sigmoid_gate))
    ).astype(BF16)
    pre_up_ref[...] = (grad_hidden * silu_gate).astype(BF16)
    total = jnp.broadcast_to(
        jnp.sum(hidden * grad_hidden, axis=1, keepdims=True), gate_sum_ref.shape
    )

    @pl.when(pl.program_id(0) == 0)
    def _():
        gate_sum_ref[...] = total

    @pl.when(pl.program_id(0) > 0)
    def _():
        gate_sum_ref[...] += total


def grads_kernel(
    inputs_ref, scaled_ref, hidden_ref, pre_gate_ref, pre_up_ref, gate_ref, up_ref, gate_sum_ref,
    back_ref, weight_ref,
):
    hid = hidden_ref.shape[1]
    step = inputs_ref.shape[1]
    at = pl.multiple_of(pl.program_id(0) * step, step)
    pre_gate, pre_up = pre_gate_ref[...], pre_up_ref[...]
    back_ref[:, pl.ds(at, step)] = (
        dot(pre_gate, gate_ref[...], 1, 1) + dot(pre_up, up_ref[...], 1, 1)
    ).astype(BF16)
    inputs = inputs_ref[...]
    weight_ref[:, :hid] = dot(inputs, pre_gate, 0, 0).astype(BF16)
    weight_ref[:, hid : 2 * hid] = dot(inputs, pre_up, 0, 0).astype(BF16)
    weight_ref[:, 2 * hid :] = dot(scaled_ref[...], hidden_ref[...], 0, 0).astype(BF16)

    @pl.when(pl.program_id(0) == 0)
    def _():
        back_ref[:, back_ref.shape[1] - LANES :] = gate_sum_ref[...].astype(BF16)


def home_kernel(target_ref, gates_ref, back_ref, grads_ref, gate_grads_ref):
    slots, count = back_ref.shape[0], target_ref.shape[1]
    width = grads_ref.shape[1]
    slot = lax.broadcasted_iota(jnp.int32, (slots, count), 0)
    from_first = jnp.where(slot == target_ref[0:1, :], 1.0, 0.0).astype(BF16)
    from_second = jnp.where(slot == target_ref[1:2, :], 1.0, 0.0).astype(BF16)
    both = from_first + from_second
    step = 512
    for at in range(0, width, step):
        grads_ref[:, at : at + step] = dot(both, back_ref[:, at : at + step], 0, 0).astype(BF16)
    sums = back_ref[:, width:]
    first = dot(sums, from_first, 0, 0)[0:1, :]
    second = dot(sums, from_second, 0, 0)[0:1, :]
    gates = gates_ref[...].astype(F32)
    gate_grads_ref[0:1, :] = (first / gates[0:1, :]).astype(BF16)
    gate_grads_ref[1:2, :] = (second / gates[1:2, :]).astype(BF16)


def whole(shape):
    return pl.BlockSpec(shape, lambda i: (0,) * len(shape))


def shards(tokens, grad_out, expert_ids, gates, gate_up_weight, down_weight):
    count, top = expert_ids.shape
    width = tokens.shape[1]
    experts = lax.axis_size("blk")
    capacity = 2 * count * top // experts
    slots = experts * capacity
    gate_up, down = gate_up_weight[0], down_weight[0]
    hid = down.shape[1]
    ids_t, gates_t = expert_ids.T, gates.T
    params = functools.partial(pltpu.CompilerParams, vmem_limit_bytes=48 * MIB)

    send, target = pl.pallas_call(
        functools.partial(dispatch_kernel, experts=experts),
        out_shape=(
            jax.ShapeDtypeStruct((slots, 2 * width), BF16),
            jax.ShapeDtypeStruct((top, count), jnp.int32),
        ),
        compiler_params=params(),
        name="dispatch",
    )(ids_t, gates_t, tokens, grad_out)

    rows = lax.all_to_all(
        send.reshape(experts, capacity, 2 * width), "blk", split_axis=0, concat_axis=0, tiled=True
    ).reshape(slots, 2 * width)

    tile = 256
    steps = hid // tile
    hidden, pre_gate, pre_up, gate_sum = pl.pallas_call(
        rows_kernel,
        grid=(steps,),
        in_specs=[
            whole((slots, 2 * width)),
            pl.BlockSpec((width, tile), lambda i: (0, i)),
            pl.BlockSpec((width, tile), lambda i: (0, steps + i)),
            pl.BlockSpec((width, tile), lambda i: (0, i)),
        ],
        out_specs=[pl.BlockSpec((slots, tile), lambda i: (0, i))] * 3 + [whole((slots, LANES))],
        out_shape=[jax.ShapeDtypeStruct((slots, hid), BF16)] * 3
        + [jax.ShapeDtypeStruct((slots, LANES), F32)],
        compiler_params=params(),
        name="rows",
    )(rows, gate_up, gate_up, down)

    tile = 512
    steps = width // tile
    back, weight = pl.pallas_call(
        grads_kernel,
        grid=(steps,),
        in_specs=[
            pl.BlockSpec((slots, tile), lambda i: (0, i)),
            pl.BlockSpec((slots, tile), lambda i: (0, steps + i)),
            whole((slots, hid)),
            whole((slots, hid)),
            whole((slots, hid)),
            pl.BlockSpec((tile, hid), lambda i: (i, 0)),
            pl.BlockSpec((tile, hid), lambda i: (i, 1)),
            whole((slots, LANES)),
        ],
        out_specs=[whole((slots, width + LANES)), pl.BlockSpec((tile, 3 * hid), lambda i: (i, 0))],
        out_shape=[
            jax.ShapeDtypeStruct((slots, width + LANES), BF16),
            jax.ShapeDtypeStruct((width, 3 * hid), BF16),
        ],
        compiler_params=params(),
        name="grads",
    )(rows, rows, hidden, pre_gate, pre_up, gate_up, gate_up, gate_sum)

    weight_total = lax.psum_scatter(weight, "rep", scatter_dimension=0, tiled=True).astype(F32)
    returned = lax.all_to_all(
        back.reshape(experts, capacity, width + LANES), "blk", split_axis=0, concat_axis=0, tiled=True
    ).reshape(slots, width + LANES)

    grad_tokens, gate_grads = pl.pallas_call(
        home_kernel,
        out_shape=(
            jax.ShapeDtypeStruct((count, width), BF16),
            jax.ShapeDtypeStruct((top, count), BF16),
        ),
        compiler_params=params(),
        name="home",
    )(target, gates_t, returned)
    return (
        grad_tokens,
        gate_grads.T,
        weight_total[None, :, : 2 * hid],
        weight_total[None, :, 2 * hid :],
    )


def solution(mesh):
    in_specs = (
        P(("blk", "rep"), None),
        P(("blk", "rep"), None),
        P(("blk", "rep"), None),
        P(("blk", "rep"), None),
        P("blk", None, None),
        P("blk", None, None),
    )
    out_specs = (
        P(("blk", "rep"), None),
        P(("blk", "rep"), None),
        P("blk", "rep", None),
        P("blk", "rep", None),
    )
    return jax.shard_map(shards, mesh=mesh, in_specs=in_specs, out_specs=out_specs, check_vma=False)
```

time: 377 us -> 231 us (0.61)
  waiting for transfers between devices: 216 us -> 0.02 us
  blocking collectives: 35.3 us -> 186 us
  matrix products: 38.3 us -> 0 us
  starting transfers between devices: 27 us -> 0.04 us
  local copies, waits for them, and re-layouts: 31.2 us -> 5.15 us
  Pallas kernels: 0 us -> 24.4 us
  other arithmetic: 14.7 us -> 1.14 us
    all_to_all x1 -> x2, blocking collectives: 35.3 us -> 186 us  [the longest x1 127 us: shards(): lax.all_to_all(back.reshape(experts, capacity, width + LANES), 'blk', spl...]
    reduce_scatter x2 -> x1, waiting for transfers between devices: 129 us -> 0.01 us  [shards(): lax.psum_scatter(weight, 'rep', scatter_dimension=0, tiled=True).astype(F32)]
    all_to_all x4 -> x0, waiting for transfers between devices: 86.3 us -> none  [the longest x1 66.5 us: shards(): lax.all_to_all(row_grad.reshape(experts, capacity, model_width), 'blk', s...]
    dot_general x6 -> x0, matrix products: 38.3 us -> none  [the longest x2 14.5 us: outer_sum(): lax.dot_general(left_rows, right_rows, (((0,), (0,)), ((), ())), preferre...]
    all_to_all x4 -> x0, starting transfers between devices: 26.8 us -> none  [the longest x1 8.45 us: shards(): lax.all_to_all(send_gates, 'blk', split_axis=0, concat_axis=0, tiled=True)]
    pallas_call x0 -> x4, Pallas kernels: none -> 24.4 us  [the longest x1 12.6 us: shards(): pl.pallas_call(grads_kernel, grid=(steps,), in_specs=[pl.BlockSpec((slots...]
    gather x5 -> x0, local copies, waits for them, and re-layouts: 23.3 us -> none  [the longest x1 6.43 us: shards(): grad_out[token_of]]
    reduce_sum x3 -> x0, other arithmetic: 4.81 us -> none  [the longest x1 4.57 us: shards(): jnp.sum(per_row.reshape(token_count, top_count, model_width).astype(jnp.f...]
  transfers between devices with their start and end apart: 6 -> 1, of which waited for: 3 -> 0; matrix products, arithmetic and copies ran while one was open for 17% -> 0% of each run, Pallas kernels for 0% -> 1%
where the time goes in v1:
time: 231 us
  blocking collectives  186 us (81%)
  Pallas kernels  24.4 us (11%)
  between operations  14.1 us (6%)
  local copies, waits for them, and re-layouts  5.15 us (2%)
    all_to_all x1, blocking collectives, shards(): lax.all_to_all(back.reshape(experts, capacity, width + LANES), 'blk', spl...  127 us
    all_to_all x1, blocking collectives, shards(): lax.all_to_all(send.reshape(experts, capacity, 2 * width), 'blk', split_a...  59.1 us
    pallas_call x1, Pallas kernels, shards(): pl.pallas_call(grads_kernel, grid=(steps,), in_specs=[pl.BlockSpec((slots...  12.6 us
    pallas_call x1, Pallas kernels, shards(): pl.pallas_call(rows_kernel, grid=(steps,), in_specs=[whole((slots, 2 * wi...  9.03 us
  transfers between devices with their start and end apart: 1, of which 0 were waited for; matrix products, arithmetic and copies ran while one was open for 0% of the time, Pallas kernels for 1%

profile of v1, /device:TPU:1, one launch (start us, length us, event | category | flops | bytes accessed | tf_op | source)
XLA Modules:
  0.0 230.6 jit_solution(12764436181009030048)
XLA Ops:
  7.2 0.0 reduce-scatter.2.cloned.1.call-start
  7.2 0.0 copy-start.1
  7.2 1.0 copy-done.1
  8.3 0.0 copy-start.2
  8.3 1.0 copy-done.2
  9.3 0.0 copy-start.3
  9.3 0.7 copy-done.3
  10.0 0.0 copy-start.5
  10.0 0.7 copy-done.5
  10.6 1.4 dispatch.1
  12.0 0.0 copy-start
  12.1 59.1 %all_to_all.10 = bf16[16,32,4096]{2,1,0:T(8,128)(2,1)} all-to-all(bf16[16,32,4096]{2,1,0:T(8,128)(2,1)S(1)} %bitcast.14), channel_id=1, replica_groups=mesh['blk'=16,'rep'=16] {'blk'}, dimensions={0} | all-to-all | bytes 8388608 | tf_op jit(solution)/shard_map/all_to_all | solution.py:153
  71.1 0.0 copy-done
  71.1 9.0 %rows.1 = (bf16[512,768]{1,0:T(8,128)(2,1)S(1)}, bf16[512,768]{1,0:T(8,128)(2,1)S(1)}, bf16[512,768]{1,0:T(8,128)(2,1)S(1)}, f32[512,128]{1,0:T(8,128)S(1)}) custom-call(bf16[512,4096]{1,0:T(8,128)(2,1)} %bitcast.24, bf16[2048,1536]{1,0:T(8,128)(2,1)} %bitcast.20, bf16[2048,1536]{1,0:T(8,128)(2,1)} %bitcast.21, bf16[2048,768]{1,0:T(8,128)(2,1)S(1)} %bitcast.15), custom_call_target="tpu_custom_call" | custom-call | tf_op jit(solution)/shard_map/rows/pallas_call | solution.py:159
  80.2 12.6 %grads.1 = (bf16[512,2176]{1,0:T(8,128)(2,1)S(1)}, bf16[2048,2304]{1,0:T(8,128)(2,1)}) custom-call(bf16[512,4096]{1,0:T(8,128)(2,1)} %bitcast.25, bf16[512,4096]{1,0:T(8,128)(2,1)} %bitcast.26, bf16[512,768]{1,0:T(8,128)(2,1)S(1)} %get-tuple-element.16.hidden_ref, bf16[512,768]{1,0:T(8,128)(2,1)S(1)} %get-tuple-element.17.pre_gate_ref, ...), custom_call_target="tpu_custom_call" | custom-call | tf_op jit(solution)/shard_map/grads/pallas_call | solution.py:177
  92.8 0.0 reduce-scatter.2.cloned.1.call-update
  92.8 0.0 copy-start.4
  92.8 126.7 %all_to_all.11 = bf16[16,32,2176]{2,1,0:T(8,128)(2,1)S(1)} all-to-all(bf16[16,32,2176]{2,1,0:T(8,128)(2,1)S(1)} %bitcast.16), channel_id=1, replica_groups=mesh['blk'=16,'rep'=16] {'blk'}, dimensions={0} | all-to-all | bytes 4456448 | tf_op jit(solution)/shard_map/all_to_all | solution.py:200
  219.5 0.0 copy-done.4
  219.5 1.3 home.1
  220.8 0.0 reduce-scatter.2.cloned.1.call-done
  220.8 1.1 convert_element_type.3
  222.0 0.8 slice_bitcast_fusion.1
  222.8 1.0 slice_bitcast_fusion
Async XLA Ops:
  7.2 213.7 %reduce-scatter.2.cloned.1.call-start = ((), (), s32[]{:S(2)}) async-start(), calls=%async_computation.3 | async-start | bytes 10027008 | tf_op jit(solution)/shard_map/reduce_scatter | solution.py:199
  7.2 1.0 copy-start.1
  8.3 1.0 copy-start.2
  9.3 0.7 copy-start.3
  10.0 0.7 copy-start.5
  12.0 59.1 %copy-start = (bf16[1,2048,768]{2,1,0:T(8,128)(2,1)S(1)}, bf16[1,2048,768]{2,1,0:T(8,128)(2,1)}, u32[]{:S(2)}) copy-start(bf16[1,2048,768]{2,1,0:T(8,128)(2,1)} %param.11) | copy-start | bytes 9437188
  92.8 126.7 %copy-start.4 = (bf16[128,2]{0,1:T(2,128)(2,1)S(1)}, bf16[128,2]{0,1:T(2,128)(2,1)}, u32[]{:S(2)}) copy-start(bf16[128,2]{0,1:T(2,128)(2,1)} %param.9) | copy-start | bytes 1540
Sparse Core Ops, SparseCore 0:
  92.9 123.7 reduce-scatter.1

commit v2 on v1

--- a/solution.py
+++ b/solution.py
@@ -9,8 +9,9 @@
 
 BF16 = jnp.bfloat16
 F32 = jnp.float32
-LANES = 128
+LANES = 256
 MIB = 1024 * 1024
+TOTAL_COST = 5_000_000_000
 
 
 def dot(left, right, left_dim=1, right_dim=0):
@@ -19,7 +20,12 @@
     )
 
 
-def dispatch_kernel(ids_ref, gates_ref, tokens_ref, grads_ref, send_ref, target_ref, *, experts):
+def dispatch_kernel(
+    ids_ref, gates_ref, tokens_ref, grads_ref, send_ref, target_ref, place_ref, *, experts, ring
+):
+    rep = lax.axis_index("rep")
+    place_ref[0] = lax.rem(rep, ring)
+    place_ref[1] = lax.div(rep, ring)
     count = ids_ref.shape[1]
     slots = send_ref.shape[0]
     width = tokens_ref.shape[1]
@@ -86,28 +92,79 @@
         gate_sum_ref[...] += total
 
 
-def grads_kernel(
-    inputs_ref, scaled_ref, hidden_ref, pre_gate_ref, pre_up_ref, gate_ref, up_ref, gate_sum_ref,
-    back_ref, weight_ref,
-):
-    hid = hidden_ref.shape[1]
-    step = inputs_ref.shape[1]
+def row_grads_kernel(place_ref, pre_gate_ref, pre_up_ref, gate_ref, up_ref, gate_sum_ref, back_ref):
+    step = gate_ref.shape[0]
     at = pl.multiple_of(pl.program_id(0) * step, step)
-    pre_gate, pre_up = pre_gate_ref[...], pre_up_ref[...]
     back_ref[:, pl.ds(at, step)] = (
-        dot(pre_gate, gate_ref[...], 1, 1) + dot(pre_up, up_ref[...], 1, 1)
+        dot(pre_gate_ref[...], gate_ref[...], 1, 1) + dot(pre_up_ref[...], up_ref[...], 1, 1)
     ).astype(BF16)
-    inputs = inputs_ref[...]
-    weight_ref[:, :hid] = dot(inputs, pre_gate, 0, 0).astype(BF16)
-    weight_ref[:, hid : 2 * hid] = dot(inputs, pre_up, 0, 0).astype(BF16)
-    weight_ref[:, 2 * hid :] = dot(scaled_ref[...], hidden_ref[...], 0, 0).astype(BF16)
 
     @pl.when(pl.program_id(0) == 0)
     def _():
         back_ref[:, back_ref.shape[1] - LANES :] = gate_sum_ref[...].astype(BF16)
 
 
-def home_kernel(target_ref, gates_ref, back_ref, grads_ref, gate_grads_ref):
+def add(*terms):
+    return sum([term.astype(F32) for term in terms])
+
+
+def terms_kernel(place_ref, hidden_ref, pre_gate_ref, pre_up_ref, *refs, groups):
+    operands = iter(refs[: len(refs) - len(groups)])
+    hid = hidden_ref.shape[1]
+
+    def first(inputs, scaled, own):
+        return (dot(inputs, pre_gate_ref[...], 0, 0), dot(inputs, pre_up_ref[:, :own], 0, 0))
+
+    def last(inputs, scaled, own):
+        return (dot(inputs, pre_up_ref[:, own:], 0, 0), dot(scaled, hidden_ref[...], 0, 0))
+
+    for (items, kind), out_ref in zip(groups, refs[len(refs) - len(groups) :]):
+        part = out_ref.shape[-1]
+        own = part - hid
+        loaded = [
+            (next(operands)[...], None if of_first else next(operands)[...])
+            + tuple(next(operands) for _ in range(added))
+            for _, _, of_first, added in items
+        ]
+        paired = len(items) == 2 and items[0][2] == items[1][2]
+        if paired:
+            inputs = jnp.concatenate([loaded[0][0], loaded[1][0]], axis=1)
+            scaled = None if items[0][2] else jnp.concatenate([loaded[0][1], loaded[1][1]], axis=1)
+            sums = (first if items[0][2] else last)(inputs, scaled, own)
+            rows = inputs.shape[1] // 2
+            results = [tuple(half[:rows] for half in sums), tuple(half[rows:] for half in sums)]
+        else:
+            results = [
+                (first if item[2] else last)(load[0], load[1], own)
+                for item, load in zip(items, loaded)
+            ]
+        for at, (item, load, result) in enumerate(zip(items, loaded, results)):
+            start = 0
+            for piece in result:
+                end = start + piece.shape[1]
+                for added in load[2:]:
+                    piece = piece + added[0, :, start:end].astype(F32)
+                out_ref[at, :, start:end] = piece.astype(kind)
+                start = end
+
+
+def joined_kernel(place_ref, kept_ref, other_ref, up_out, down_out):
+    up_out[0] = add(kept_ref[0], other_ref[0]).astype(BF16)
+    down_out[0] = add(kept_ref[1], other_ref[1]).astype(BF16)
+
+
+def total_kernel(
+    place_ref, base_ref, x_up_ref, x_down_ref, y_up_ref, y_down_ref, gate_up_ref, down_ref
+):
+    part = x_up_ref.shape[-1]
+    wide = gate_up_ref.shape[-1]
+    last = add(base_ref[1], x_down_ref[0], y_up_ref[0])
+    gate_up_ref[0, :, :part] = add(base_ref[0], x_up_ref[0], y_down_ref[0])
+    gate_up_ref[0, :, part:] = last[:, : wide - part]
+    down_ref[0] = last[:, wide - part :]
+
+
+def home_kernel(target_ref, gates_ref, back_ref, after_ref, grads_ref, gate_grads_ref):
     slots, count = back_ref.shape[0], target_ref.shape[1]
     width = grads_ref.shape[1]
     slot = lax.broadcasted_iota(jnp.int32, (slots, count), 0)
@@ -117,7 +174,7 @@
     step = 512
     for at in range(0, width, step):
         grads_ref[:, at : at + step] = dot(both, back_ref[:, at : at + step], 0, 0).astype(BF16)
-    sums = back_ref[:, width:]
+    sums = back_ref[:, width : width + 128]
     first = dot(sums, from_first, 0, 0)[0:1, :]
     second = dot(sums, from_second, 0, 0)[0:1, :]
     gates = gates_ref[...].astype(F32)
@@ -138,15 +195,22 @@
     gate_up, down = gate_up_weight[0], down_weight[0]
     hid = down.shape[1]
     ids_t, gates_t = expert_ids.T, gates.T
+    ring = lax.axis_size("rep") // 2
     params = functools.partial(pltpu.CompilerParams, vmem_limit_bytes=48 * MIB)
 
-    send, target = pl.pallas_call(
-        functools.partial(dispatch_kernel, experts=experts),
+    send, target, place = pl.pallas_call(
+        functools.partial(dispatch_kernel, experts=experts, ring=ring),
         out_shape=(
             jax.ShapeDtypeStruct((slots, 2 * width), BF16),
             jax.ShapeDtypeStruct((top, count), jnp.int32),
+            jax.ShapeDtypeStruct((2,), jnp.int32),
         ),
-        compiler_params=params(),
+        out_specs=(
+            pl.BlockSpec(memory_space=pltpu.VMEM),
+            pl.BlockSpec(memory_space=pltpu.VMEM),
+            pl.BlockSpec(memory_space=pltpu.SMEM),
+        ),
+        compiler_params=params(vmem_limit_bytes=60 * MIB),
         name="dispatch",
     )(ids_t, gates_t, tokens, grad_out)
 
@@ -172,31 +236,206 @@
         name="rows",
     )(rows, gate_up, gate_up, down)
 
-    tile = 512
+    block = width // lax.axis_size("rep")
+
+    def around(place, ahead):
+        return lax.rem(place[0] + ahead, ring)
+
+    def whole_p(shape):
+        return pl.BlockSpec(shape, lambda i, p: (0,) * len(shape))
+
+    anywhere = pl.BlockSpec(memory_space=pl.ANY)
+
+    def call(kernel, name, grid, in_specs, out_specs, out_shape, *operands, after=(), cost=1):
+        first = 1 + len(in_specs)
+
+        def body(*refs):
+            kernel(*refs[:first], *refs[first + len(after) : -1])
+            refs[-1][...] = jnp.zeros_like(refs[-1])
+
+        *outs, token = pl.pallas_call(
+            body,
+            grid_spec=pltpu.PrefetchScalarGridSpec(
+                num_scalar_prefetch=1,
+                grid=(grid,),
+                in_specs=[*in_specs, *[anywhere] * len(after)],
+                out_specs=[*out_specs, whole_p((8, 128))],
+            ),
+            out_shape=[*out_shape, jax.ShapeDtypeStruct((8, 128), F32)],
+            compiler_params=params(),
+            cost_estimate=pl.CostEstimate(flops=cost, bytes_accessed=1, transcendentals=0),
+            name=name,
+        )(place, *operands, *after)
+        return outs, token
+
+    def shape(*dims):
+        return pltpu.HBM(dims, BF16)
+
+    def permute(array, ahead):
+        pairs = [
+            (high * ring + low, high * ring + (low + ahead) % ring)
+            for high in range(2)
+            for low in range(ring)
+        ]
+        return lax.ppermute(array, "rep", pairs)
+
+    def swap(array):
+        pairs = [(at, (at + ring) % (2 * ring)) for at in range(2 * ring)]
+        return lax.ppermute(array, "rep", pairs)
+
+    far = ring // 2
+    part = 3 * hid // 2
+
+    def onward(pair):
+        return permute(pair[0], 1), permute(pair[1], -1)
+
+    def some_terms(name, groups, after=()):
+        specs, operands, counted, outs, kinds = [], [], [], [], []
+        for items, kind in groups:
+            for half, ahead, of_first, added in items:
+                for start in (0,) if of_first else (0, 2):
+
+                    def at(i, p, half=half, ahead=ahead, start=start):
+                        return 0, (start + half(p)) * ring + around(p, (ahead + ring) % ring)
+
+                    specs.append(pl.BlockSpec((slots, block), at))
+                    operands.append(rows)
+                for array, place_of in added:
+
+                    def at(i, p, place_of=place_of):
+                        return place_of(p), 0, 0
+
+                    specs.append(pl.BlockSpec((1, block, part), at))
+                    operands.append(array)
+            counted.append(([item[:3] + (len(item[3]),) for item in items], kind))
+            outs.append(whole_p((len(items), block, part)))
+            kinds.append(
+                shape(len(items), block, part)
+                if kind == BF16
+                else jax.ShapeDtypeStruct((len(items), block, part), kind)
+            )
+        return call(
+            functools.partial(terms_kernel, groups=counted),
+            name,
+            1,
+            [whole_p((slots, hid))] * 3 + specs,
+            outs,
+            kinds,
+            hidden, pre_gate, pre_up, *operands, after=after,
+        )
+
+    def low(p):
+        return 0
+
+    def high(p):
+        return 1
+
+    def mine(p):
+        return p[1]
+
+    def theirs(p):
+        return 1 - p[1]
+
+    def hop(name, at, up_first, pair, after):
+        def both(ahead, of_first, array):
+            return [
+                (half, ahead, of_first, [] if array is None else [(array, half)])
+                for half in (low, high)
+            ], BF16
+
+        up, down = pair or (None, None)
+        return some_terms(
+            name, [both(at, up_first, up), both(-at, not up_first, down)], after
+        )
+
+    def split_hop(name, at, up_first, pair, after):
+        def one_half(half, kind):
+            return [
+                (half, at, up_first, [(pair[0], half)]),
+                (half, -at, not up_first, [(pair[1], half)]),
+            ], kind
+
+        return some_terms(name, [one_half(mine, F32), one_half(theirs, BF16)], after)
+
+    one = whole_p((1, block, part))
+    pair_of = whole_p((2, block, part))
+
+    def joined(name, kept, other, after):
+        return call(
+            joined_kernel,
+            name,
+            1,
+            [pair_of, pair_of],
+            [one] * 2,
+            [shape(1, block, part)] * 2,
+            kept, other, after=after,
+        )
+
+    tile = 4 * block
     steps = width // tile
-    back, weight = pl.pallas_call(
-        grads_kernel,
-        grid=(steps,),
-        in_specs=[
-            pl.BlockSpec((slots, tile), lambda i: (0, i)),
-            pl.BlockSpec((slots, tile), lambda i: (0, steps + i)),
-            whole((slots, hid)),
-            whole((slots, hid)),
-            whole((slots, hid)),
-            pl.BlockSpec((tile, hid), lambda i: (i, 0)),
-            pl.BlockSpec((tile, hid), lambda i: (i, 1)),
-            whole((slots, LANES)),
+    (sent,), token = some_terms(
+        "own_theirs", [([(theirs, 0, True, []), (theirs, 0, False, [])], BF16)]
+    )
+    own_other = swap(sent)
+    sent, token = hop("first_x", far, True, None, (token,))
+    x_pair = onward(sent)
+    sent, token = hop("first_y", far - 1, False, None, (token,))
+    y_pair = onward(sent)
+    (base,), token = some_terms(
+        "own",
+        [
+            (
+                [
+                    (mine, 0, True, [(own_other, low)]),
+                    (mine, 0, False, [(own_other, high)]),
+                ],
+                F32,
+            )
         ],
-        out_specs=[whole((slots, width + LANES)), pl.BlockSpec((tile, 3 * hid), lambda i: (i, 0))],
-        out_shape=[
-            jax.ShapeDtypeStruct((slots, width + LANES), BF16),
-            jax.ShapeDtypeStruct((width, 3 * hid), BF16),
+        (token,),
+    )
+    (back,), token = call(
+        row_grads_kernel,
+        "row_grads",
+        steps,
+        [
+            whole_p((slots, hid)),
+            whole_p((slots, hid)),
+            pl.BlockSpec((tile, hid), lambda i, p: (i, 0)),
+            pl.BlockSpec((tile, hid), lambda i, p: (i, 1)),
+            whole_p((slots, LANES)),
         ],
-        compiler_params=params(),
-        name="grads",
-    )(rows, rows, hidden, pre_gate, pre_up, gate_up, gate_up, gate_sum)
-
-    weight_total = lax.psum_scatter(weight, "rep", scatter_dimension=0, tiled=True).astype(F32)
+        [whole_p((slots, width + LANES))],
+        [shape(slots, width + LANES)],
+        pre_gate, pre_up, gate_up, gate_up, gate_sum, after=(token,),
+    )
+    sent, token = hop("hop_x3", far - 1, True, x_pair, (token,))
+    x_pair = onward(sent)
+    sent, token = hop("hop_y2", far - 2, False, y_pair, (token,))
+    y_pair = onward(sent)
+    sent, token = hop("hop_x2", far - 2, True, x_pair, (token,))
+    x_pair = onward(sent)
+    (y_kept, sent), token = split_hop("hop_y1", far - 3, False, y_pair, (token,))
+    y_other = swap(sent)
+    (x_kept, sent), token = split_hop("hop_x1", far - 3, True, x_pair, (token,))
+    x_other = swap(sent)
+    sent, token = joined("joined_y", y_kept, y_other, (token,))
+    y_pair = onward(sent)
+    sent, token = joined("joined_x", x_kept, x_other, (token,))
+    x_pair = onward(sent)
+    (gate_up_total, down_total), token = call(
+        total_kernel,
+        "total",
+        1,
+        [pair_of, one, one, one, one],
+        [whole_p((1, block, 2 * hid)), whole_p((1, block, hid))],
+        [
+            jax.ShapeDtypeStruct((1, block, 2 * hid), F32),
+            jax.ShapeDtypeStruct((1, block, hid), F32),
+        ],
+        base, *x_pair, *y_pair, cost=TOTAL_COST,
+    )
+
     returned = lax.all_to_all(
         back.reshape(experts, capacity, width + LANES), "blk", split_axis=0, concat_axis=0, tiled=True
     ).reshape(slots, width + LANES)
@@ -209,13 +448,8 @@
         ),
         compiler_params=params(),
         name="home",
-    )(target, gates_t, returned)
-    return (
-        grad_tokens,
-        gate_grads.T,
-        weight_total[None, :, : 2 * hid],
-        weight_total[None, :, 2 * hid :],
-    )
+    )(target, gates_t, returned, token)
+    return grad_tokens, gate_grads.T, gate_up_total, down_total
 
 
 def solution(mesh):

time: 231 us -> 189 us (0.82); the launches traced: 231 us -> 186 us
  blocking collectives: 186 us -> 59.3 us
  waiting for transfers between devices: 0.02 us -> 35.6 us
  Pallas kernels: 24.4 us -> 59.1 us
  starting transfers between devices: 0.04 us -> 30.8 us
  between operations: 14.1 us -> 0.73 us
  local copies, waits for them, and re-layouts: 5.15 us -> 0.03 us
    all_to_all x1 -> x0, blocking collectives: 127 us -> none  [shards(): lax.all_to_all(back.reshape(experts, capacity, width + LANES), 'blk', spl...]
    ppermute x0 -> x17, waiting for transfers between devices: none -> 35.6 us  [the longest x14 22.6 us: permute(): return lax.ppermute(array, 'rep', pairs)]
    pallas_call x2 -> x14, Pallas kernels: 14 us -> 47 us  [the longest x13 42.3 us: call(): pl.pallas_call(body, grid_spec=pltpu.PrefetchScalarGridSpec(num_scalar_pr...]
    ppermute x0 -> x17, starting transfers between devices: none -> 24.1 us  [the longest x14 21.7 us: permute(): return lax.ppermute(array, 'rep', pairs)]
    all_to_all x0 -> x1, starting transfers between devices: none -> 6.71 us  [shards(): lax.all_to_all(back.reshape(experts, capacity, width + LANES), 'blk', spl...]
    unnamed x12, local copies, waits for them, and re-layouts: 3.42 us -> 0.03 us
  transfers between devices with their start and end apart: 1 -> 18, of which waited for: 0 -> 7; matrix products, arithmetic and copies ran while one was open for 0% -> 0% of each run, Pallas kernels for 1% -> 21%
where the time goes in v2:
time: 189 us; the launch traced here: 186 us
  blocking collectives  59.3 us (31%)
  Pallas kernels  59.1 us (31%)
  waiting for transfers between devices  35.6 us (19%)
  starting transfers between devices  30.8 us (16%)
    all_to_all x1, blocking collectives, shards(): lax.all_to_all(send.reshape(experts, capacity, 2 * width), 'blk', split_a...  59.3 us
    pallas_call x13, Pallas kernels, call(): pl.pallas_call(body, grid_spec=pltpu.PrefetchScalarGridSpec(num_scalar_pr...  42.3 us
    ppermute x14, waiting for transfers between devices, permute(): return lax.ppermute(array, 'rep', pairs)  22.6 us
    ppermute x14, starting transfers between devices, permute(): return lax.ppermute(array, 'rep', pairs)  21.7 us
    ppermute x3, waiting for transfers between devices, swap(): return lax.ppermute(array, 'rep', pairs)  13.1 us
    pallas_call x1, Pallas kernels, shards(): pl.pallas_call(rows_kernel, grid=(steps,), in_specs=[whole((slots, 2 * wi...  9.09 us
    all_to_all x1, starting transfers between devices, shards(): lax.all_to_all(back.reshape(experts, capacity, width + LANES), 'blk', spl...  6.71 us
    pallas_call x1, Pallas kernels, shards(): pl.pallas_call(functools.partial(dispatch_kernel, experts=experts, ring=r...  4.69 us
  transfers between devices with their start and end apart: 18, of which 7 were waited for; matrix products, arithmetic and copies ran while one was open for 0% of the time, Pallas kernels for 21%

profile of v2, /device:TPU:1, one launch (start us, length us, event | category | flops | bytes accessed | tf_op | source)
XLA Modules:
  0.0 185.6 jit_solution(3245046176588476046)
XLA Ops:
  0.6 4.7 %dispatch.1 = (bf16[512,4096]{1,0:T(8,128)(2,1)}, s32[2,128]{1,0:T(2,128)}, s32[2]{0:T(128)}) custom-call(s32[2,128]{1,0:T(2,128)} %bitcast.67, bf16[2,128]{1,0:T(2,128)(2,1)} %bitcast.10, bf16[128,2048]{1,0:T(8,128)(2,1)} %tokens_ref.1, bf16[128,2048]{1,0:T(8,128)(2,1)} %grads_ref.1), custom_call_target="tpu_custom_call" | custom-call | tf_op jit(solution)/shard_map/dispatch/pallas_call | solution.py:201
  5.3 0.0 copy-start
  5.3 59.3 %all_to_all.10 = bf16[16,32,4096]{2,1,0:T(8,128)(2,1)} all-to-all(bf16[16,32,4096]{2,1,0:T(8,128)(2,1)} %bitcast.65), channel_id=1, replica_groups=mesh['blk'=16,'rep'=16] {'blk'}, dimensions={0} | all-to-all | bytes 8388608 | tf_op jit(solution)/shard_map/all_to_all | solution.py:217
  64.6 0.0 copy-done
  64.6 0.0 copy-start.1
  64.6 9.1 %rows.1 = (bf16[512,768]{1,0:T(8,128)(2,1)S(1)}, bf16[512,768]{1,0:T(8,128)(2,1)S(1)}, bf16[512,768]{1,0:T(8,128)(2,1)S(1)}, f32[512,256]{1,0:T(8,128)S(1)}) custom-call(bf16[512,4096]{1,0:T(8,128)(2,1)} %bitcast.12, bf16[2048,1536]{1,0:T(8,128)(2,1)} %bitcast.61, bf16[2048,1536]{1,0:T(8,128)(2,1)} %bitcast.62, bf16[2048,768]{1,0:T(8,128)(2,1)S(1)} %bitcast.9), custom_call_target="tpu_custom_call" | custom-call | tf_op jit(solution)/shard_map/rows/pallas_call | solution.py:223
  73.7 0.0 copy-done.1
  73.7 3.0 %own_theirs.1 = (bf16[2,128,1152]{2,1,0:T(8,128)(2,1)}, f32[8,128]{1,0:T(8,128)S(1)}) custom-call(s32[2]{0:T(128)S(1)} %copy-done.1, bf16[512,768]{1,0:T(8,128)(2,1)S(1)} %get-tuple-element.54.refs_1_, bf16[512,768]{1,0:T(8,128)(2,1)S(1)} %get-tuple-element.51.refs_2_.refs_1_, bf16[512,768]{1,0:T(8,128)(2,1)S(1)} %get-tuple-element.52.refs_3_.refs_2_, ...), custom_call_target="tpu_custom_call" | custom-call | flops 1 | bytes 1 | tf_op jit(solution)/shard_map/own_theirs/pallas_call | solution.py:256
  76.7 0.4 collective-permute-start
  77.1 3.5 %first_x.1 = (bf16[2,128,1152]{2,1,0:T(8,128)(2,1)}, bf16[2,128,1152]{2,1,0:T(8,128)(2,1)}, f32[8,128]{1,0:T(8,128)S(1)}) custom-call(s32[2]{0:T(128)S(1)} %copy-done.1, bf16[512,768]{1,0:T(8,128)(2,1)S(1)} %get-tuple-element.54.refs_1_, bf16[512,768]{1,0:T(8,128)(2,1)S(1)} %get-tuple-element.51.refs_2_.refs_1_, ...), custom_call_target="tpu_custom_call" | custom-call | flops 1 | bytes 1 | tf_op jit(solution)/shard_map/first_x/pallas_call | solution.py:256
  80.6 1.6 collective-permute-start.1
  82.2 3.9 %collective-permute-start.2 = (bf16[2,128,1152]{2,1,0:T(8,128)(2,1)}, bf16[2,128,1152]{2,1,0:T(8,128)(2,1)S(1)}, u32[]{:S(2)}, u32[]{:S(2)}) collective-permute-start(bf16[2,128,1152]{2,1,0:T(8,128)(2,1)} %get-tuple-element.63), channel_id=1, source_target_pairs={{0,7},{1,0},{2,1},{3,2},{4,3},{5,4},{6,5},{7,6},{8,15},{9,8},{10,9... | collective-permute-start | bytes 1769480 | tf_op jit(solution)/shard_map/ppermute | solution.py:280
  86.2 3.5 %first_y.1 = (bf16[2,128,1152]{2,1,0:T(8,128)(2,1)}, bf16[2,128,1152]{2,1,0:T(8,128)(2,1)}, f32[8,128]{1,0:T(8,128)S(1)}) custom-call(s32[2]{0:T(128)S(1)} %copy-done.1, bf16[512,768]{1,0:T(8,128)(2,1)S(1)} %get-tuple-element.54.refs_1_, bf16[512,768]{1,0:T(8,128)(2,1)S(1)} %get-tuple-element.51.refs_2_.refs_1_, ...), custom_call_target="tpu_custom_call" | custom-call | flops 1 | bytes 1 | tf_op jit(solution)/shard_map/first_y/pallas_call | solution.py:256
  89.7 0.0 collective-permute-start.5
  89.7 2.7 %collective-permute-start.6 = (bf16[2,128,1152]{2,1,0:T(8,128)(2,1)}, bf16[2,128,1152]{2,1,0:T(8,128)(2,1)S(1)}, u32[]{:S(2)}, u32[]{:S(2)}) collective-permute-start(bf16[2,128,1152]{2,1,0:T(8,128)(2,1)} %get-tuple-element.68), channel_id=1, source_target_pairs={{0,7},{1,0},{2,1},{3,2},{4,3},{5,4},{6,5},{7,6},{8,15},{9,8},{10,9... | collective-permute-start | bytes 1769480 | tf_op jit(solution)/shard_map/ppermute | solution.py:280
  92.4 0.0 collective-permute-done.refs_5_.refs_8_
  92.4 2.1 %own.1 = (f32[2,128,1152]{2,1,0:T(8,128)S(1)}, f32[8,128]{1,0:T(8,128)S(1)}) custom-call(s32[2]{0:T(128)S(1)} %copy-done.1, bf16[512,768]{1,0:T(8,128)(2,1)S(1)} %get-tuple-element.54.refs_1_, bf16[512,768]{1,0:T(8,128)(2,1)S(1)} %get-tuple-element.51.refs_2_.refs_1_, bf16[512,768]{1,0:T(8,128)(2,1)S(1)} %get-tuple-element.52.refs_3_.refs_2_, ...), custom_call_target="tpu_custom_call" | custom-call | flops 1 | bytes 1 | tf_op jit(solution)/shard_map/own/pallas_call | solution.py:256
  94.5 0.0 copy-start.4
  94.5 7.9 %row_grads.1 = (bf16[512,2304]{1,0:T(8,128)(2,1)}, f32[8,128]{1,0:T(8,128)S(1)}) custom-call(s32[2]{0:T(128)S(1)} %copy-done.1, bf16[512,768]{1,0:T(8,128)(2,1)S(1)} %get-tuple-element.51.refs_2_.refs_1_, bf16[512,768]{1,0:T(8,128)(2,1)S(1)} %get-tuple-element.52.refs_3_.refs_2_, bf16[2048,1536]{1,0:T(8,128)(2,1)} %bitcast.63, bf16[2048,1536]{1,0:T(8,128)(2,1)} %bitcast.64, ...), custom_call_target="tpu_custom_call" | custom-call | flops 1 | bytes 1 | tf_op jit(solution)/shard_map/row_grads/pallas_call | solution.py:256
  102.4 0.0 copy-done.4
  102.4 0.0 collective-permute-done.1.refs_5_.refs_7_
  102.4 0.0 collective-permute-done.2.refs_10_.refs_13_
  102.4 3.5 %hop_x3.1 = (bf16[2,128,1152]{2,1,0:T(8,128)(2,1)}, bf16[2,128,1152]{2,1,0:T(8,128)(2,1)}, f32[8,128]{1,0:T(8,128)S(1)}) custom-call(s32[2]{0:T(128)S(1)} %copy-done.1, bf16[512,768]{1,0:T(8,128)(2,1)S(1)} %get-tuple-element.54.refs_1_, bf16[512,768]{1,0:T(8,128)(2,1)S(1)} %get-tuple-element.51.refs_2_.refs_1_, ...), custom_call_target="tpu_custom_call" | custom-call | flops 1 | bytes 1 | tf_op jit(solution)/shard_map/hop_x3/pallas_call | solution.py:256
  106.0 0.0 collective-permute-start.3
  106.0 3.6 %collective-permute-start.4 = (bf16[2,128,1152]{2,1,0:T(8,128)(2,1)}, bf16[2,128,1152]{2,1,0:T(8,128)(2,1)}, u32[]{:S(2)}, u32[]{:S(2)}) collective-permute-start(bf16[2,128,1152]{2,1,0:T(8,128)(2,1)} %get-tuple-element.66), channel_id=1, source_target_pairs={{0,7},{1,0},{2,1},{3,2},{4,3},{5,4},{6,5},{7,6},{8,15},{9,8},{10,9... | collective-permute-start | bytes 1769480 | tf_op jit(solution)/shard_map/ppermute | solution.py:280
  109.6 6.7 %all-to-all-start.1 = ((bf16[16,32,2304]{2,1,0:T(8,128)(2,1)}), bf16[16,32,2304]{2,1,0:T(8,128)(2,1)}, u32[]{:S(2)}, u32[]{:S(2)}) async-start(bf16[16,32,2304]{2,1,0:T(8,128)(2,1)} %bitcast.66), calls=%async_computation.1 | async-start | bytes 4718592 | tf_op jit(solution)/shard_map/all_to_all | solution.py:439
  116.3 0.0 collective-permute-done.5.refs_6_.refs_9_
  116.3 0.0 collective-permute-done.6.refs_11_.refs_13_
  116.3 3.5 %hop_y2.1 = (bf16[2,128,1152]{2,1,0:T(8,128)(2,1)}, bf16[2,128,1152]{2,1,0:T(8,128)(2,1)}, f32[8,128]{1,0:T(8,128)S(1)}) custom-call(s32[2]{0:T(128)S(1)} %copy-done.1, bf16[512,768]{1,0:T(8,128)(2,1)S(1)} %get-tuple-element.54.refs_1_, bf16[512,768]{1,0:T(8,128)(2,1)S(1)} %get-tuple-element.51.refs_2_.refs_1_, ...), custom_call_target="tpu_custom_call" | custom-call | flops 1 | bytes 1 | tf_op jit(solution)/shard_map/hop_y2/pallas_call | solution.py:256
  119.8 1.7 collective-permute-start.10
  121.5 0.0 collective-permute-start.9
  121.5 2.3 %collective-permute-done.3.refs_5_.refs_7_ = bf16[2,128,1152]{2,1,0:T(8,128)(2,1)} collective-permute-done((bf16[2,128,1152]{2,1,0:T(8,128)(2,1)}, bf16[2,128,1152]{2,1,0:T(8,128)(2,1)}, u32[]{:S(2)}, u32[]{:S(2)}) %collective-permute-start.3) | collective-permute-done | bytes 589856 | tf_op jit(solution)/shard_map/ppermute | solution.py:280
  123.8 0.0 collective-permute-done.4.refs_10_.refs_13_
  123.8 3.8 %hop_x2.1 = (bf16[2,128,1152]{2,1,0:T(8,128)(2,1)}, bf16[2,128,1152]{2,1,0:T(8,128)(2,1)}, f32[8,128]{1,0:T(8,128)S(1)}) custom-call(s32[2]{0:T(128)S(1)} %copy-done.1, bf16[512,768]{1,0:T(8,128)(2,1)S(1)} %get-tuple-element.54.refs_1_, bf16[512,768]{1,0:T(8,128)(2,1)S(1)} %get-tuple-element.51.refs_2_.refs_1_, ...), custom_call_target="tpu_custom_call" | custom-call | flops 1 | bytes 1 | tf_op jit(solution)/shard_map/hop_x2/pallas_call | solution.py:256
  127.6 0.0 collective-permute-start.7
  127.6 2.7 %collective-permute-start.8 = (bf16[2,128,1152]{2,1,0:T(8,128)(2,1)}, bf16[2,128,1152]{2,1,0:T(8,128)(2,1)S(1)}, u32[]{:S(2)}, u32[]{:S(2)}) collective-permute-start(bf16[2,128,1152]{2,1,0:T(8,128)(2,1)} %get-tuple-element.72), channel_id=1, source_target_pairs={{0,7},{1,0},{2,1},{3,2},{4,3},{5,4},{6,5},{7,6},{8,15},{9,8},{10,9... | collective-permute-start | bytes 1769480 | tf_op jit(solution)/shard_map/ppermute | solution.py:280
  130.3 5.4 %collective-permute-done.10.refs_8_.refs_13_ = bf16[2,128,1152]{2,1,0:T(8,128)(2,1)S(1)} collective-permute-done((bf16[2,128,1152]{2,1,0:T(8,128)(2,1)}, bf16[2,128,1152]{2,1,0:T(8,128)(2,1)S(1)}, u32[]{:S(2)}, u32[]{:S(2)}) %collective-permute-start.10) | collective-permute-done | bytes 589856 | tf_op jit(solution)/shard_map/ppermute | solution.py:280
  135.7 1.5 collective-permute-done.9.refs_6_.refs_11_
  137.3 3.5 %hop_y1.1 = (f32[2,128,1152]{2,1,0:T(8,128)S(1)}, bf16[2,128,1152]{2,1,0:T(8,128)(2,1)}, f32[8,128]{1,0:T(8,128)S(1)}) custom-call(s32[2]{0:T(128)S(1)} %copy-done.1, bf16[512,768]{1,0:T(8,128)(2,1)S(1)} %get-tuple-element.54.refs_1_, bf16[512,768]{1,0:T(8,128)(2,1)S(1)} %get-tuple-element.51.refs_2_.refs_1_, ...), custom_call_target="tpu_custom_call" | custom-call | flops 1 | bytes 1 | tf_op jit(solution)/shard_map/hop_y1/pallas_call | solution.py:256
  140.8 1.0 collective-permute-start.12
  141.8 8.1 %collective-permute-done.7.refs_5_.refs_10_ = bf16[2,128,1152]{2,1,0:T(8,128)(2,1)S(1)} collective-permute-done((bf16[2,128,1152]{2,1,0:T(8,128)(2,1)}, bf16[2,128,1152]{2,1,0:T(8,128)(2,1)S(1)}, u32[]{:S(2)}, u32[]{:S(2)}) %collective-permute-start.7) | collective-permute-done | bytes 589856 | tf_op jit(solution)/shard_map/ppermute | solution.py:280
  149.9 0.0 collective-permute-done.8.refs_8_.refs_13_
  149.9 3.5 %hop_x1.1 = (f32[2,128,1152]{2,1,0:T(8,128)S(1)}, bf16[2,128,1152]{2,1,0:T(8,128)(2,1)}, f32[8,128]{1,0:T(8,128)S(1)}) custom-call(s32[2]{0:T(128)S(1)} %copy-done.1, bf16[512,768]{1,0:T(8,128)(2,1)S(1)} %get-tuple-element.54.refs_1_, bf16[512,768]{1,0:T(8,128)(2,1)S(1)} %get-tuple-element.51.refs_2_.refs_1_, ...), custom_call_target="tpu_custom_call" | custom-call | flops 1 | bytes 1 | tf_op jit(solution)/shard_map/hop_x1/pallas_call | solution.py:256
  153.4 0.0 copy-start.5
  153.4 1.0 collective-permute-start.11
  154.4 4.5 %collective-permute-done.12.refs_2_ = bf16[2,128,1152]{2,1,0:T(8,128)(2,1)S(1)} collective-permute-done((bf16[2,128,1152]{2,1,0:T(8,128)(2,1)}, bf16[2,128,1152]{2,1,0:T(8,128)(2,1)S(1)}, u32[]{:S(2)}, u32[]{:S(2)}) %collective-permute-start.12) | collective-permute-done | bytes 589856 | tf_op jit(solution)/shard_map/ppermute | solution.py:284
  159.0 1.4 joined_y.1
  160.4 0.0 collective-permute-start.15
  160.4 2.7 %collective-permute-start.16 = (bf16[1,128,1152]{2,1,0:T(8,128)(2,1)}, bf16[1,128,1152]{2,1,0:T(8,128)(2,1)S(1)}, u32[]{:S(2)}, u32[]{:S(2)}) collective-permute-start(bf16[1,128,1152]{2,1,0:T(8,128)(2,1)} %get-tuple-element.86), channel_id=1, source_target_pairs={{0,7},{1,0},{2,1},{3,2},{4,3},{5,4},{6,5},{7,6},{8,15},{9,8},{10,9... | collective-permute-start | bytes 884744 | tf_op jit(solution)/shard_map/ppermute | solution.py:280
  163.1 8.5 %collective-permute-done.11.refs_2_ = bf16[2,128,1152]{2,1,0:T(8,128)(2,1)S(1)} collective-permute-done((bf16[2,128,1152]{2,1,0:T(8,128)(2,1)}, bf16[2,128,1152]{2,1,0:T(8,128)(2,1)S(1)}, u32[]{:S(2)}, u32[]{:S(2)}) %collective-permute-start.11) | collective-permute-done | bytes 589856 | tf_op jit(solution)/shard_map/ppermute | solution.py:284
  171.6 1.4 joined_x.1
  173.0 0.0 collective-permute-start.13
  173.0 2.7 %collective-permute-start.14 = (bf16[1,128,1152]{2,1,0:T(8,128)(2,1)}, bf16[1,128,1152]{2,1,0:T(8,128)(2,1)S(1)}, u32[]{:S(2)}, u32[]{:S(2)}) collective-permute-start(bf16[1,128,1152]{2,1,0:T(8,128)(2,1)} %get-tuple-element.84), channel_id=1, source_target_pairs={{0,7},{1,0},{2,1},{3,2},{4,3},{5,4},{6,5},{7,6},{8,15},{9,8},{10,9... | collective-permute-start | bytes 884744 | tf_op jit(solution)/shard_map/ppermute | solution.py:280
  175.7 0.0 collective-permute-done.15.refs_4_
  175.7 0.0 collective-permute-done.16.refs_5_
  175.7 5.2 %collective-permute-done.13.refs_2_ = bf16[1,128,1152]{2,1,0:T(8,128)(2,1)S(1)} collective-permute-done((bf16[1,128,1152]{2,1,0:T(8,128)(2,1)}, bf16[1,128,1152]{2,1,0:T(8,128)(2,1)S(1)}, u32[]{:S(2)}, u32[]{:S(2)}) %collective-permute-start.13) | collective-permute-done | bytes 294944 | tf_op jit(solution)/shard_map/ppermute | solution.py:280
  180.9 0.0 collective-permute-done.14.refs_3_
  180.9 0.0 copy-done.5
  180.9 0.0 copy-start.3
  180.9 1.7 total.1
  182.6 0.0 all-to-all-done.1
  182.6 0.0 copy-done.2
  182.6 0.0 copy-done.3
  182.6 3.0 %home.1 = (bf16[128,2048]{1,0:T(8,128)(2,1)}, bf16[2,128]{1,0:T(2,128)(2,1)}) custom-call(s32[2,128]{1,0:T(2,128)S(1)} %copy-done.3, bf16[2,128]{1,0:T(2,128)(2,1)S(1)} %bitcast.11, bf16[512,2304]{1,0:T(8,128)(2,1)} %bitcast.7.back_ref, f32[8,128]{1,0:T(8,128)S(1)} %get-tuple-element.87.after_ref), custom_call_target="tpu_custom_call" | custom-call | tf_op jit(solution)/shard_map/home/pallas_call | solution.py:443
  (1 shorter events, 0.0 us)
Async XLA Ops:
  5.3 59.3 %copy-start = (bf16[1,2048,768]{2,1,0:T(8,128)(2,1)S(1)}, bf16[1,2048,768]{2,1,0:T(8,128)(2,1)}, u32[]{:S(2)}) copy-start(bf16[1,2048,768]{2,1,0:T(8,128)(2,1)} %param.11) | copy-start | bytes 9437188
  64.6 9.1 %copy-start.1 = (s32[2]{0:T(128)S(1)}, s32[2]{0:T(128)}, u32[]{:S(2)}) copy-start(s32[2]{0:T(128)} %get-tuple-element.49.refs_0_) | copy-start | bytes 28
  76.7 15.7 %collective-permute-start = (bf16[2,128,1152]{2,1,0:T(8,128)(2,1)}, bf16[2,128,1152]{2,1,0:T(8,128)(2,1)S(1)}, u32[]{:S(2)}, u32[]{:S(2)}) collective-permute-start(bf16[2,128,1152]{2,1,0:T(8,128)(2,1)} %get-tuple-element.55), channel_id=1, source_target_pairs={{0,8},{1,9},{2,10},{3,11},{4,12},{5,13},{6,14},{7,15},{8,0},{9,1},... | collective-permute-start | bytes 1769480 | tf_op jit(solution)/shard_map/ppermute | solution.py:284
  80.6 21.8 %collective-permute-start.1 = (bf16[2,128,1152]{2,1,0:T(8,128)(2,1)}, bf16[2,128,1152]{2,1,0:T(8,128)(2,1)S(1)}, u32[]{:S(2)}, u32[]{:S(2)}) collective-permute-start(bf16[2,128,1152]{2,1,0:T(8,128)(2,1)} %get-tuple-element.62), channel_id=1, source_target_pairs={{0,1},{1,2},{2,3},{3,4},{4,5},{5,6},{6,7},{7,0},{8,9},{9,10},{10,1... | collective-permute-start | bytes 1769480 | tf_op jit(solution)/shard_map/ppermute | solution.py:280
  82.2 20.2 %collective-permute-start.2 = (bf16[2,128,1152]{2,1,0:T(8,128)(2,1)}, bf16[2,128,1152]{2,1,0:T(8,128)(2,1)S(1)}, u32[]{:S(2)}, u32[]{:S(2)}) collective-permute-start(bf16[2,128,1152]{2,1,0:T(8,128)(2,1)} %get-tuple-element.63), channel_id=1, source_target_pairs={{0,7},{1,0},{2,1},{3,2},{4,3},{5,4},{6,5},{7,6},{8,15},{9,8},{10,9... | collective-permute-start | bytes 1769480 | tf_op jit(solution)/shard_map/ppermute | solution.py:280
  89.7 26.6 %collective-permute-start.5 = (bf16[2,128,1152]{2,1,0:T(8,128)(2,1)}, bf16[2,128,1152]{2,1,0:T(8,128)(2,1)S(1)}, u32[]{:S(2)}, u32[]{:S(2)}) collective-permute-start(bf16[2,128,1152]{2,1,0:T(8,128)(2,1)} %get-tuple-element.67), channel_id=1, source_target_pairs={{0,1},{1,2},{2,3},{3,4},{4,5},{5,6},{6,7},{7,0},{8,9},{9,10},{10,1... | collective-permute-start | bytes 1769480 | tf_op jit(solution)/shard_map/ppermute | solution.py:280
  89.7 26.6 %collective-permute-start.6 = (bf16[2,128,1152]{2,1,0:T(8,128)(2,1)}, bf16[2,128,1152]{2,1,0:T(8,128)(2,1)S(1)}, u32[]{:S(2)}, u32[]{:S(2)}) collective-permute-start(bf16[2,128,1152]{2,1,0:T(8,128)(2,1)} %get-tuple-element.68), channel_id=1, source_target_pairs={{0,7},{1,0},{2,1},{3,2},{4,3},{5,4},{6,5},{7,6},{8,15},{9,8},{10,9... | collective-permute-start | bytes 1769480 | tf_op jit(solution)/shard_map/ppermute | solution.py:280
  94.5 7.9 %copy-start.4 = (f32[2,128,1152]{2,1,0:T(8,128)}, f32[2,128,1152]{2,1,0:T(8,128)S(1)}, u32[]{:S(2)}) copy-start(f32[2,128,1152]{2,1,0:T(8,128)S(1)} %get-tuple-element.61.refs_1_) | copy-start | bytes 3538948
  106.0 17.8 %collective-permute-start.3 = (bf16[2,128,1152]{2,1,0:T(8,128)(2,1)}, bf16[2,128,1152]{2,1,0:T(8,128)(2,1)}, u32[]{:S(2)}, u32[]{:S(2)}) collective-permute-start(bf16[2,128,1152]{2,1,0:T(8,128)(2,1)} %get-tuple-element.65), channel_id=1, source_target_pairs={{0,1},{1,2},{2,3},{3,4},{4,5},{5,6},{6,7},{7,0},{8,9},{9,10},{10,1... | collective-permute-start | bytes 1769480 | tf_op jit(solution)/shard_map/ppermute | solution.py:280
  106.0 17.8 %collective-permute-start.4 = (bf16[2,128,1152]{2,1,0:T(8,128)(2,1)}, bf16[2,128,1152]{2,1,0:T(8,128)(2,1)}, u32[]{:S(2)}, u32[]{:S(2)}) collective-permute-start(bf16[2,128,1152]{2,1,0:T(8,128)(2,1)} %get-tuple-element.66), channel_id=1, source_target_pairs={{0,7},{1,0},{2,1},{3,2},{4,3},{5,4},{6,5},{7,6},{8,15},{9,8},{10,9... | collective-permute-start | bytes 1769480 | tf_op jit(solution)/shard_map/ppermute | solution.py:280
  109.6 73.0 %all-to-all-start.1 = ((bf16[16,32,2304]{2,1,0:T(8,128)(2,1)}), bf16[16,32,2304]{2,1,0:T(8,128)(2,1)}, u32[]{:S(2)}, u32[]{:S(2)}) async-start(bf16[16,32,2304]{2,1,0:T(8,128)(2,1)} %bitcast.66), calls=%async_computation.1 | async-start | bytes 4718592 | tf_op jit(solution)/shard_map/all_to_all | solution.py:439
  119.8 16.0 %collective-permute-start.10 = (bf16[2,128,1152]{2,1,0:T(8,128)(2,1)}, bf16[2,128,1152]{2,1,0:T(8,128)(2,1)S(1)}, u32[]{:S(2)}, u32[]{:S(2)}) collective-permute-start(bf16[2,128,1152]{2,1,0:T(8,128)(2,1)} %get-tuple-element.74), channel_id=1, source_target_pairs={{0,7},{1,0},{2,1},{3,2},{4,3},{5,4},{6,5},{7,6},{8,15},{9,8},{10,9... | collective-permute-start | bytes 1769480 | tf_op jit(solution)/shard_map/ppermute | solution.py:280
  121.5 15.7 %collective-permute-start.9 = (bf16[2,128,1152]{2,1,0:T(8,128)(2,1)}, bf16[2,128,1152]{2,1,0:T(8,128)(2,1)S(1)}, u32[]{:S(2)}, u32[]{:S(2)}) collective-permute-start(bf16[2,128,1152]{2,1,0:T(8,128)(2,1)} %get-tuple-element.73), channel_id=1, source_target_pairs={{0,1},{1,2},{2,3},{3,4},{4,5},{5,6},{6,7},{7,0},{8,9},{9,10},{10,1... | collective-permute-start | bytes 1769480 | tf_op jit(solution)/shard_map/ppermute | solution.py:280
  127.6 22.3 %collective-permute-start.7 = (bf16[2,128,1152]{2,1,0:T(8,128)(2,1)}, bf16[2,128,1152]{2,1,0:T(8,128)(2,1)S(1)}, u32[]{:S(2)}, u32[]{:S(2)}) collective-permute-start(bf16[2,128,1152]{2,1,0:T(8,128)(2,1)} %get-tuple-element.71), channel_id=1, source_target_pairs={{0,1},{1,2},{2,3},{3,4},{4,5},{5,6},{6,7},{7,0},{8,9},{9,10},{10,1... | collective-permute-start | bytes 1769480 | tf_op jit(solution)/shard_map/ppermute | solution.py:280
  127.6 22.3 %collective-permute-start.8 = (bf16[2,128,1152]{2,1,0:T(8,128)(2,1)}, bf16[2,128,1152]{2,1,0:T(8,128)(2,1)S(1)}, u32[]{:S(2)}, u32[]{:S(2)}) collective-permute-start(bf16[2,128,1152]{2,1,0:T(8,128)(2,1)} %get-tuple-element.72), channel_id=1, source_target_pairs={{0,7},{1,0},{2,1},{3,2},{4,3},{5,4},{6,5},{7,6},{8,15},{9,8},{10,9... | collective-permute-start | bytes 1769480 | tf_op jit(solution)/shard_map/ppermute | solution.py:280
  140.8 18.2 %collective-permute-start.12 = (bf16[2,128,1152]{2,1,0:T(8,128)(2,1)}, bf16[2,128,1152]{2,1,0:T(8,128)(2,1)S(1)}, u32[]{:S(2)}, u32[]{:S(2)}) collective-permute-start(bf16[2,128,1152]{2,1,0:T(8,128)(2,1)} %get-tuple-element.80), channel_id=1, source_target_pairs={{0,8},{1,9},{2,10},{3,11},{4,12},{5,13},{6,14},{7,15},{8,0},{9,1},... | collective-permute-start | bytes 1769480 | tf_op jit(solution)/shard_map/ppermute | solution.py:284
  153.4 27.5 %copy-start.5 = (f32[2,128,1152]{2,1,0:T(8,128)S(1)}, f32[2,128,1152]{2,1,0:T(8,128)}, u32[]{:S(2)}) copy-start(f32[2,128,1152]{2,1,0:T(8,128)} %copy-done.4) | copy-start | bytes 3538948
  153.4 18.2 %collective-permute-start.11 = (bf16[2,128,1152]{2,1,0:T(8,128)(2,1)}, bf16[2,128,1152]{2,1,0:T(8,128)(2,1)S(1)}, u32[]{:S(2)}, u32[]{:S(2)}) collective-permute-start(bf16[2,128,1152]{2,1,0:T(8,128)(2,1)} %get-tuple-element.78), channel_id=1, source_target_pairs={{0,8},{1,9},{2,10},{3,11},{4,12},{5,13},{6,14},{7,15},{8,0},{9,1},... | collective-permute-start | bytes 1769480 | tf_op jit(solution)/shard_map/ppermute | solution.py:284
  160.4 15.3 %collective-permute-start.15 = (bf16[1,128,1152]{2,1,0:T(8,128)(2,1)}, bf16[1,128,1152]{2,1,0:T(8,128)(2,1)S(1)}, u32[]{:S(2)}, u32[]{:S(2)}) collective-permute-start(bf16[1,128,1152]{2,1,0:T(8,128)(2,1)} %get-tuple-element.85), channel_id=1, source_target_pairs={{0,1},{1,2},{2,3},{3,4},{4,5},{5,6},{6,7},{7,0},{8,9},{9,10},{10,1... | collective-permute-start | bytes 884744 | tf_op jit(solution)/shard_map/ppermute | solution.py:280
  160.4 15.3 %collective-permute-start.16 = (bf16[1,128,1152]{2,1,0:T(8,128)(2,1)}, bf16[1,128,1152]{2,1,0:T(8,128)(2,1)S(1)}, u32[]{:S(2)}, u32[]{:S(2)}) collective-permute-start(bf16[1,128,1152]{2,1,0:T(8,128)(2,1)} %get-tuple-element.86), channel_id=1, source_target_pairs={{0,7},{1,0},{2,1},{3,2},{4,3},{5,4},{6,5},{7,6},{8,15},{9,8},{10,9... | collective-permute-start | bytes 884744 | tf_op jit(solution)/shard_map/ppermute | solution.py:280
  173.0 7.9 %collective-permute-start.13 = (bf16[1,128,1152]{2,1,0:T(8,128)(2,1)}, bf16[1,128,1152]{2,1,0:T(8,128)(2,1)S(1)}, u32[]{:S(2)}, u32[]{:S(2)}) collective-permute-start(bf16[1,128,1152]{2,1,0:T(8,128)(2,1)} %get-tuple-element.83), channel_id=1, source_target_pairs={{0,1},{1,2},{2,3},{3,4},{4,5},{5,6},{6,7},{7,0},{8,9},{9,10},{10,1... | collective-permute-start | bytes 884744 | tf_op jit(solution)/shard_map/ppermute | solution.py:280
  173.0 7.9 %collective-permute-start.14 = (bf16[1,128,1152]{2,1,0:T(8,128)(2,1)}, bf16[1,128,1152]{2,1,0:T(8,128)(2,1)S(1)}, u32[]{:S(2)}, u32[]{:S(2)}) collective-permute-start(bf16[1,128,1152]{2,1,0:T(8,128)(2,1)} %get-tuple-element.84), channel_id=1, source_target_pairs={{0,7},{1,0},{2,1},{3,2},{4,3},{5,4},{6,5},{7,6},{8,15},{9,8},{10,9... | collective-permute-start | bytes 884744 | tf_op jit(solution)/shard_map/ppermute | solution.py:280
  180.9 1.7 copy-start.2
  180.9 1.7 copy-start.3

commit v3 on v2

--- a/solution.py
+++ b/solution.py
@@ -9,7 +9,7 @@
 
 BF16 = jnp.bfloat16
 F32 = jnp.float32
-LANES = 256
+LANES = 128
 MIB = 1024 * 1024
 TOTAL_COST = 5_000_000_000
 
@@ -164,7 +164,7 @@
     down_ref[0] = last[:, wide - part :]
 
 
-def home_kernel(target_ref, gates_ref, back_ref, after_ref, grads_ref, gate_grads_ref):
+def home_kernel(target_ref, gates_ref, back_ref, grads_ref, gate_grads_ref):
     slots, count = back_ref.shape[0], target_ref.shape[1]
     width = grads_ref.shape[1]
     slot = lax.broadcasted_iota(jnp.int32, (slots, count), 0)
@@ -360,7 +360,7 @@
     one = whole_p((1, block, part))
     pair_of = whole_p((2, block, part))
 
-    def joined(name, kept, other, after):
+    def joined(name, kept, other, after, cost=1):
         return call(
             joined_kernel,
             name,
@@ -368,32 +368,20 @@
             [pair_of, pair_of],
             [one] * 2,
             [shape(1, block, part)] * 2,
-            kept, other, after=after,
+            kept, other, after=after, cost=cost,
         )
 
     tile = 4 * block
     steps = width // tile
+    sent, token = hop("first_x", far, True, None, ())
+    x_pair = onward(sent)
     (sent,), token = some_terms(
-        "own_theirs", [([(theirs, 0, True, []), (theirs, 0, False, [])], BF16)]
+        "own_theirs", [([(theirs, 0, True, []), (theirs, 0, False, [])], BF16)],
+        (token,),
     )
     own_other = swap(sent)
-    sent, token = hop("first_x", far, True, None, (token,))
-    x_pair = onward(sent)
     sent, token = hop("first_y", far - 1, False, None, (token,))
     y_pair = onward(sent)
-    (base,), token = some_terms(
-        "own",
-        [
-            (
-                [
-                    (mine, 0, True, [(own_other, low)]),
-                    (mine, 0, False, [(own_other, high)]),
-                ],
-                F32,
-            )
-        ],
-        (token,),
-    )
     (back,), token = call(
         row_grads_kernel,
         "row_grads",
@@ -413,6 +401,19 @@
     x_pair = onward(sent)
     sent, token = hop("hop_y2", far - 2, False, y_pair, (token,))
     y_pair = onward(sent)
+    (base,), token = some_terms(
+        "own",
+        [
+            (
+                [
+                    (mine, 0, True, [(own_other, low)]),
+                    (mine, 0, False, [(own_other, high)]),
+                ],
+                F32,
+            )
+        ],
+        (token,),
+    )
     sent, token = hop("hop_x2", far - 2, True, x_pair, (token,))
     x_pair = onward(sent)
     (y_kept, sent), token = split_hop("hop_y1", far - 3, False, y_pair, (token,))
@@ -421,9 +422,9 @@
     x_other = swap(sent)
     sent, token = joined("joined_y", y_kept, y_other, (token,))
     y_pair = onward(sent)
-    sent, token = joined("joined_x", x_kept, x_other, (token,))
+    sent, token = joined("joined_x", x_kept, x_other, (token,), TOTAL_COST)
     x_pair = onward(sent)
-    (gate_up_total, down_total), token = call(
+    (gate_up_total, down_total), _ = call(
         total_kernel,
         "total",
         1,
@@ -433,7 +434,7 @@
             jax.ShapeDtypeStruct((1, block, 2 * hid), F32),
             jax.ShapeDtypeStruct((1, block, hid), F32),
         ],
-        base, *x_pair, *y_pair, cost=TOTAL_COST,
+        base, *x_pair, *y_pair,
     )
 
     returned = lax.all_to_all(
@@ -448,7 +449,7 @@
         ),
         compiler_params=params(),
         name="home",
-    )(target, gates_t, returned, token)
+    )(target, gates_t, returned)
     return grad_tokens, gate_grads.T, gate_up_total, down_total
 
 

time: 189 us -> 182 us (0.963)
  waiting for transfers between devices: 35.6 us -> 29.7 us
    ppermute x14, waiting for transfers between devices: 22.6 us -> 16.1 us  [permute(): return lax.ppermute(array, 'rep', pairs)]
  transfers between devices with their start and end apart: 18 -> 18, of which waited for: 7 -> 5; matrix products, arithmetic and copies ran while one was open for 0% -> 0% of each run, Pallas kernels for 21% -> 22%
where the time goes in v3:
time: 182 us; the launch traced here: 180 us
  Pallas kernels  59.3 us (33%)
  blocking collectives  59.3 us (33%)
  starting transfers between devices  30.2 us (17%)
  waiting for transfers between devices  29.7 us (16%)
    all_to_all x1, blocking collectives, shards(): lax.all_to_all(send.reshape(experts, capacity, 2 * width), 'blk', split_a...  59.3 us
    pallas_call x13, Pallas kernels, call(): pl.pallas_call(body, grid_spec=pltpu.PrefetchScalarGridSpec(num_scalar_pr...  42.6 us
    ppermute x14, starting transfers between devices, permute(): return lax.ppermute(array, 'rep', pairs)  21.6 us
    ppermute x14, waiting for transfers between devices, permute(): return lax.ppermute(array, 'rep', pairs)  16.1 us
    ppermute x3, waiting for transfers between devices, swap(): return lax.ppermute(array, 'rep', pairs)  13.5 us
    pallas_call x1, Pallas kernels, shards(): pl.pallas_call(rows_kernel, grid=(steps,), in_specs=[whole((slots, 2 * wi...  9.05 us
    all_to_all x1, starting transfers between devices, shards(): lax.all_to_all(back.reshape(experts, capacity, width + LANES), 'blk', spl...  7.36 us
    pallas_call x1, Pallas kernels, shards(): pl.pallas_call(functools.partial(dispatch_kernel, experts=experts, ring=r...  4.69 us
  transfers between devices with their start and end apart: 18, of which 5 were waited for; matrix products, arithmetic and copies ran while one was open for 0% of the time, Pallas kernels for 22%

profile of v3, /device:TPU:1, one launch (start us, length us, event | category | flops | bytes accessed | tf_op | source)
XLA Modules:
  0.0 180.2 jit_solution(167928224610427399)
XLA Ops:
  0.6 4.7 %dispatch.1 = (bf16[512,4096]{1,0:T(8,128)(2,1)}, s32[2,128]{1,0:T(2,128)}, s32[2]{0:T(128)}) custom-call(s32[2,128]{1,0:T(2,128)} %bitcast.67, bf16[2,128]{1,0:T(2,128)(2,1)} %bitcast.10, bf16[128,2048]{1,0:T(8,128)(2,1)} %tokens_ref.1, bf16[128,2048]{1,0:T(8,128)(2,1)} %grads_ref.1), custom_call_target="tpu_custom_call" | custom-call | tf_op jit(solution)/shard_map/dispatch/pallas_call | solution.py:201
  5.3 0.0 copy-start
  5.3 59.3 %all_to_all.10 = bf16[16,32,4096]{2,1,0:T(8,128)(2,1)} all-to-all(bf16[16,32,4096]{2,1,0:T(8,128)(2,1)} %bitcast.65), channel_id=1, replica_groups=mesh['blk'=16,'rep'=16] {'blk'}, dimensions={0} | all-to-all | bytes 8388608 | tf_op jit(solution)/shard_map/all_to_all | solution.py:217
  64.6 0.0 copy-done
  64.6 0.0 copy-start.3
  64.6 9.0 %rows.1 = (bf16[512,768]{1,0:T(8,128)(2,1)S(1)}, bf16[512,768]{1,0:T(8,128)(2,1)S(1)}, bf16[512,768]{1,0:T(8,128)(2,1)S(1)}, f32[512,128]{1,0:T(8,128)S(1)}) custom-call(bf16[512,4096]{1,0:T(8,128)(2,1)} %bitcast.12, bf16[2048,1536]{1,0:T(8,128)(2,1)} %bitcast.61, bf16[2048,1536]{1,0:T(8,128)(2,1)} %bitcast.62, bf16[2048,768]{1,0:T(8,128)(2,1)S(1)} %bitcast.9), custom_call_target="tpu_custom_call" | custom-call | tf_op jit(solution)/shard_map/rows/pallas_call | solution.py:223
  73.7 0.0 copy-done.3
  73.7 3.5 %first_x.1 = (bf16[2,128,1152]{2,1,0:T(8,128)(2,1)}, bf16[2,128,1152]{2,1,0:T(8,128)(2,1)}, f32[8,128]{1,0:T(8,128)S(1)}) custom-call(s32[2]{0:T(128)S(1)} %copy-done.3, bf16[512,768]{1,0:T(8,128)(2,1)S(1)} %get-tuple-element.53.refs_1_, bf16[512,768]{1,0:T(8,128)(2,1)S(1)} %get-tuple-element.50.refs_2_.refs_1_, ...), custom_call_target="tpu_custom_call" | custom-call | flops 1 | bytes 1 | tf_op jit(solution)/shard_map/first_x/pallas_call | solution.py:256
  77.2 1.6 collective-permute-start.3
  78.8 3.9 %collective-permute-start.4 = (bf16[2,128,1152]{2,1,0:T(8,128)(2,1)}, bf16[2,128,1152]{2,1,0:T(8,128)(2,1)S(1)}, u32[]{:S(2)}, u32[]{:S(2)}) collective-permute-start(bf16[2,128,1152]{2,1,0:T(8,128)(2,1)} %get-tuple-element.64), channel_id=1, source_target_pairs={{0,7},{1,0},{2,1},{3,2},{4,3},{5,4},{6,5},{7,6},{8,15},{9,8},{10,9... | collective-permute-start | bytes 1769480 | tf_op jit(solution)/shard_map/ppermute | solution.py:280
  82.8 3.0 %own_theirs.1 = (bf16[2,128,1152]{2,1,0:T(8,128)(2,1)}, f32[8,128]{1,0:T(8,128)S(1)}) custom-call(s32[2]{0:T(128)S(1)} %copy-done.3, bf16[512,768]{1,0:T(8,128)(2,1)S(1)} %get-tuple-element.53.refs_1_, bf16[512,768]{1,0:T(8,128)(2,1)S(1)} %get-tuple-element.50.refs_2_.refs_1_, bf16[512,768]{1,0:T(8,128)(2,1)S(1)} %get-tuple-element.51.refs_3_.refs_2_, ...), custom_call_target="tpu_custom_call" | custom-call | flops 1 | bytes 1 | tf_op jit(solution)/shard_map/own_theirs/pallas_call | solution.py:256
  85.7 0.4 collective-permute-start
  86.1 3.6 %first_y.1 = (bf16[2,128,1152]{2,1,0:T(8,128)(2,1)}, bf16[2,128,1152]{2,1,0:T(8,128)(2,1)}, f32[8,128]{1,0:T(8,128)S(1)}) custom-call(s32[2]{0:T(128)S(1)} %copy-done.3, bf16[512,768]{1,0:T(8,128)(2,1)S(1)} %get-tuple-element.53.refs_1_, bf16[512,768]{1,0:T(8,128)(2,1)S(1)} %get-tuple-element.50.refs_2_.refs_1_, ...), custom_call_target="tpu_custom_call" | custom-call | flops 1 | bytes 1 | tf_op jit(solution)/shard_map/first_y/pallas_call | solution.py:256
  89.7 0.0 collective-permute-start.1
  89.7 2.7 %collective-permute-start.2 = (bf16[2,128,1152]{2,1,0:T(8,128)(2,1)}, bf16[2,128,1152]{2,1,0:T(8,128)(2,1)}, u32[]{:S(2)}, u32[]{:S(2)}) collective-permute-start(bf16[2,128,1152]{2,1,0:T(8,128)(2,1)} %get-tuple-element.62), channel_id=1, source_target_pairs={{0,7},{1,0},{2,1},{3,2},{4,3},{5,4},{6,5},{7,6},{8,15},{9,8},{10,9... | collective-permute-start | bytes 1769480 | tf_op jit(solution)/shard_map/ppermute | solution.py:280
  92.4 7.8 %row_grads.1 = (bf16[512,2176]{1,0:T(8,128)(2,1)}, f32[8,128]{1,0:T(8,128)S(1)}) custom-call(s32[2]{0:T(128)S(1)} %copy-done.3, bf16[512,768]{1,0:T(8,128)(2,1)S(1)} %get-tuple-element.50.refs_2_.refs_1_, bf16[512,768]{1,0:T(8,128)(2,1)S(1)} %get-tuple-element.51.refs_3_.refs_2_, bf16[2048,1536]{1,0:T(8,128)(2,1)} %bitcast.63, bf16[2048,1536]{1,0:T(8,128)(2,1)} %bitcast.64, ...), custom_call_target="tpu_custom_call" | custom-call | flops 1 | bytes 1 | tf_op jit(solution)/shard_map/row_grads/pallas_call | solution.py:256
  100.2 0.0 collective-permute-done.3.refs_5_.refs_7_
  100.2 0.0 collective-permute-done.4.refs_10_.refs_13_
  100.2 3.5 %hop_x3.1 = (bf16[2,128,1152]{2,1,0:T(8,128)(2,1)}, bf16[2,128,1152]{2,1,0:T(8,128)(2,1)}, f32[8,128]{1,0:T(8,128)S(1)}) custom-call(s32[2]{0:T(128)S(1)} %copy-done.3, bf16[512,768]{1,0:T(8,128)(2,1)S(1)} %get-tuple-element.53.refs_1_, bf16[512,768]{1,0:T(8,128)(2,1)S(1)} %get-tuple-element.50.refs_2_.refs_1_, ...), custom_call_target="tpu_custom_call" | custom-call | flops 1 | bytes 1 | tf_op jit(solution)/shard_map/hop_x3/pallas_call | solution.py:256
  103.7 0.0 collective-permute-start.5
  103.7 2.7 %collective-permute-start.6 = (bf16[2,128,1152]{2,1,0:T(8,128)(2,1)}, bf16[2,128,1152]{2,1,0:T(8,128)(2,1)}, u32[]{:S(2)}, u32[]{:S(2)}) collective-permute-start(bf16[2,128,1152]{2,1,0:T(8,128)(2,1)} %get-tuple-element.70), channel_id=1, source_target_pairs={{0,7},{1,0},{2,1},{3,2},{4,3},{5,4},{6,5},{7,6},{8,15},{9,8},{10,9... | collective-permute-start | bytes 1769480 | tf_op jit(solution)/shard_map/ppermute | solution.py:280
  106.4 7.4 %all-to-all-start.1 = ((bf16[16,32,2176]{2,1,0:T(8,128)(2,1)}), bf16[16,32,2176]{2,1,0:T(8,128)(2,1)}, u32[]{:S(2)}, u32[]{:S(2)}) async-start(bf16[16,32,2176]{2,1,0:T(8,128)(2,1)} %bitcast.66), calls=%async_computation.1 | async-start | bytes 4456448 | tf_op jit(solution)/shard_map/all_to_all | solution.py:440
  113.8 0.0 collective-permute-done.1.refs_6_.refs_9_
  113.8 0.0 collective-permute-done.2.refs_11_.refs_13_
  113.8 3.9 %hop_y2.1 = (bf16[2,128,1152]{2,1,0:T(8,128)(2,1)}, bf16[2,128,1152]{2,1,0:T(8,128)(2,1)}, f32[8,128]{1,0:T(8,128)S(1)}) custom-call(s32[2]{0:T(128)S(1)} %copy-done.3, bf16[512,768]{1,0:T(8,128)(2,1)S(1)} %get-tuple-element.53.refs_1_, bf16[512,768]{1,0:T(8,128)(2,1)S(1)} %get-tuple-element.50.refs_2_.refs_1_, ...), custom_call_target="tpu_custom_call" | custom-call | flops 1 | bytes 1 | tf_op jit(solution)/shard_map/hop_y2/pallas_call | solution.py:256
  117.7 0.0 collective-permute-start.9
  117.7 2.7 %collective-permute-start.10 = (bf16[2,128,1152]{2,1,0:T(8,128)(2,1)}, bf16[2,128,1152]{2,1,0:T(8,128)(2,1)S(1)}, u32[]{:S(2)}, u32[]{:S(2)}) collective-permute-start(bf16[2,128,1152]{2,1,0:T(8,128)(2,1)} %get-tuple-element.75), channel_id=1, source_target_pairs={{0,7},{1,0},{2,1},{3,2},{4,3},{5,4},{6,5},{7,6},{8,15},{9,8},{10,9... | collective-permute-start | bytes 1769480 | tf_op jit(solution)/shard_map/ppermute | solution.py:280
  120.4 0.0 collective-permute-done.refs_5_.refs_8_
  120.4 2.1 %own.1 = (f32[2,128,1152]{2,1,0:T(8,128)S(1)}, f32[8,128]{1,0:T(8,128)S(1)}) custom-call(s32[2]{0:T(128)S(1)} %copy-done.3, bf16[512,768]{1,0:T(8,128)(2,1)S(1)} %get-tuple-element.53.refs_1_, bf16[512,768]{1,0:T(8,128)(2,1)S(1)} %get-tuple-element.50.refs_2_.refs_1_, bf16[512,768]{1,0:T(8,128)(2,1)S(1)} %get-tuple-element.51.refs_3_.refs_2_, ...), custom_call_target="tpu_custom_call" | custom-call | flops 1 | bytes 1 | tf_op jit(solution)/shard_map/own/pallas_call | solution.py:256
  122.5 0.0 copy-start.1
  122.5 1.0 copy-done.1
  123.5 0.0 collective-permute-done.5.refs_5_.refs_7_
  123.5 0.0 collective-permute-done.6.refs_10_.refs_13_
  123.5 3.7 %hop_x2.1 = (bf16[2,128,1152]{2,1,0:T(8,128)(2,1)}, bf16[2,128,1152]{2,1,0:T(8,128)(2,1)}, f32[8,128]{1,0:T(8,128)S(1)}) custom-call(s32[2]{0:T(128)S(1)} %copy-done.3, bf16[512,768]{1,0:T(8,128)(2,1)S(1)} %get-tuple-element.53.refs_1_, bf16[512,768]{1,0:T(8,128)(2,1)S(1)} %get-tuple-element.50.refs_2_.refs_1_, ...), custom_call_target="tpu_custom_call" | custom-call | flops 1 | bytes 1 | tf_op jit(solution)/shard_map/hop_x2/pallas_call | solution.py:256
  127.2 0.0 collective-permute-start.7
  127.2 2.7 %collective-permute-start.8 = (bf16[2,128,1152]{2,1,0:T(8,128)(2,1)}, bf16[2,128,1152]{2,1,0:T(8,128)(2,1)S(1)}, u32[]{:S(2)}, u32[]{:S(2)}) collective-permute-start(bf16[2,128,1152]{2,1,0:T(8,128)(2,1)} %get-tuple-element.73), channel_id=1, source_target_pairs={{0,7},{1,0},{2,1},{3,2},{4,3},{5,4},{6,5},{7,6},{8,15},{9,8},{10,9... | collective-permute-start | bytes 1769480 | tf_op jit(solution)/shard_map/ppermute | solution.py:280
  129.9 4.5 %collective-permute-done.9.refs_6_.refs_11_ = bf16[2,128,1152]{2,1,0:T(8,128)(2,1)S(1)} collective-permute-done((bf16[2,128,1152]{2,1,0:T(8,128)(2,1)}, bf16[2,128,1152]{2,1,0:T(8,128)(2,1)S(1)}, u32[]{:S(2)}, u32[]{:S(2)}) %collective-permute-start.9) | collective-permute-done | bytes 589856 | tf_op jit(solution)/shard_map/ppermute | solution.py:280
  134.4 0.0 collective-permute-done.10.refs_8_.refs_13_
  134.4 3.5 %hop_y1.1 = (f32[2,128,1152]{2,1,0:T(8,128)S(1)}, bf16[2,128,1152]{2,1,0:T(8,128)(2,1)}, f32[8,128]{1,0:T(8,128)S(1)}) custom-call(s32[2]{0:T(128)S(1)} %copy-done.3, bf16[512,768]{1,0:T(8,128)(2,1)S(1)} %get-tuple-element.53.refs_1_, bf16[512,768]{1,0:T(8,128)(2,1)S(1)} %get-tuple-element.50.refs_2_.refs_1_, ...), custom_call_target="tpu_custom_call" | custom-call | flops 1 | bytes 1 | tf_op jit(solution)/shard_map/hop_y1/pallas_call | solution.py:256
  137.9 0.4 collective-permute-start.12
  138.3 8.7 %collective-permute-done.7.refs_5_.refs_10_ = bf16[2,128,1152]{2,1,0:T(8,128)(2,1)S(1)} collective-permute-done((bf16[2,128,1152]{2,1,0:T(8,128)(2,1)}, bf16[2,128,1152]{2,1,0:T(8,128)(2,1)S(1)}, u32[]{:S(2)}, u32[]{:S(2)}) %collective-permute-start.7) | collective-permute-done | bytes 589856 | tf_op jit(solution)/shard_map/ppermute | solution.py:280
  147.1 0.0 collective-permute-done.8.refs_8_.refs_13_
  147.1 3.5 %hop_x1.1 = (f32[2,128,1152]{2,1,0:T(8,128)S(1)}, bf16[2,128,1152]{2,1,0:T(8,128)(2,1)}, f32[8,128]{1,0:T(8,128)S(1)}) custom-call(s32[2]{0:T(128)S(1)} %copy-done.3, bf16[512,768]{1,0:T(8,128)(2,1)S(1)} %get-tuple-element.53.refs_1_, bf16[512,768]{1,0:T(8,128)(2,1)S(1)} %get-tuple-element.50.refs_2_.refs_1_, ...), custom_call_target="tpu_custom_call" | custom-call | flops 1 | bytes 1 | tf_op jit(solution)/shard_map/hop_x1/pallas_call | solution.py:256
  150.6 0.4 collective-permute-start.11
  151.0 5.0 %collective-permute-done.12.refs_2_ = bf16[2,128,1152]{2,1,0:T(8,128)(2,1)S(1)} collective-permute-done((bf16[2,128,1152]{2,1,0:T(8,128)(2,1)}, bf16[2,128,1152]{2,1,0:T(8,128)(2,1)S(1)}, u32[]{:S(2)}, u32[]{:S(2)}) %collective-permute-start.12) | collective-permute-done | bytes 589856 | tf_op jit(solution)/shard_map/ppermute | solution.py:284
  155.9 1.4 joined_y.1
  157.4 0.0 collective-permute-start.15
  157.4 2.7 %collective-permute-start.16 = (bf16[1,128,1152]{2,1,0:T(8,128)(2,1)}, bf16[1,128,1152]{2,1,0:T(8,128)(2,1)S(1)}, u32[]{:S(2)}, u32[]{:S(2)}) collective-permute-start(bf16[1,128,1152]{2,1,0:T(8,128)(2,1)} %get-tuple-element.87), channel_id=1, source_target_pairs={{0,7},{1,0},{2,1},{3,2},{4,3},{5,4},{6,5},{7,6},{8,15},{9,8},{10,9... | collective-permute-start | bytes 884744 | tf_op jit(solution)/shard_map/ppermute | solution.py:280
  160.0 8.5 %collective-permute-done.11.refs_2_ = bf16[2,128,1152]{2,1,0:T(8,128)(2,1)S(1)} collective-permute-done((bf16[2,128,1152]{2,1,0:T(8,128)(2,1)}, bf16[2,128,1152]{2,1,0:T(8,128)(2,1)S(1)}, u32[]{:S(2)}, u32[]{:S(2)}) %collective-permute-start.11) | collective-permute-done | bytes 589856 | tf_op jit(solution)/shard_map/ppermute | solution.py:284
  168.6 0.0 copy-start.4
  168.6 0.0 copy-start.5
  168.6 1.4 joined_x.1
  170.0 0.0 collective-permute-start.13
  170.0 2.7 %collective-permute-start.14 = (bf16[1,128,1152]{2,1,0:T(8,128)(2,1)}, bf16[1,128,1152]{2,1,0:T(8,128)(2,1)S(1)}, u32[]{:S(2)}, u32[]{:S(2)}) collective-permute-start(bf16[1,128,1152]{2,1,0:T(8,128)(2,1)} %get-tuple-element.85), channel_id=1, source_target_pairs={{0,7},{1,0},{2,1},{3,2},{4,3},{5,4},{6,5},{7,6},{8,15},{9,8},{10,9... | collective-permute-start | bytes 884744 | tf_op jit(solution)/shard_map/ppermute | solution.py:280
  172.7 0.0 all-to-all-done.1
  172.7 0.0 copy-done.4
  172.7 0.0 copy-done.5
  172.7 2.9 %home.1 = (bf16[128,2048]{1,0:T(8,128)(2,1)}, bf16[2,128]{1,0:T(2,128)(2,1)}) custom-call(s32[2,128]{1,0:T(2,128)S(1)} %copy-done.5, bf16[2,128]{1,0:T(2,128)(2,1)S(1)} %bitcast.11, bf16[512,2176]{1,0:T(8,128)(2,1)} %bitcast.7.back_ref), custom_call_target="tpu_custom_call" | custom-call | tf_op jit(solution)/shard_map/home/pallas_call | solution.py:444
  175.7 0.0 collective-permute-done.15.refs_4_
  175.7 0.0 collective-permute-done.16.refs_5_
  175.7 2.8 %collective-permute-done.13.refs_2_ = bf16[1,128,1152]{2,1,0:T(8,128)(2,1)S(1)} collective-permute-done((bf16[1,128,1152]{2,1,0:T(8,128)(2,1)}, bf16[1,128,1152]{2,1,0:T(8,128)(2,1)S(1)}, u32[]{:S(2)}, u32[]{:S(2)}) %collective-permute-start.13) | collective-permute-done | bytes 294944 | tf_op jit(solution)/shard_map/ppermute | solution.py:280
  178.5 0.0 collective-permute-done.14.refs_3_
  178.5 0.0 copy-done.2
  178.5 1.7 total.1
  (1 shorter events, 0.0 us)
Async XLA Ops:
  5.3 59.3 %copy-start = (bf16[1,2048,768]{2,1,0:T(8,128)(2,1)S(1)}, bf16[1,2048,768]{2,1,0:T(8,128)(2,1)}, u32[]{:S(2)}) copy-start(bf16[1,2048,768]{2,1,0:T(8,128)(2,1)} %param.11) | copy-start | bytes 9437188
  64.6 9.1 %copy-start.3 = (s32[2]{0:T(128)S(1)}, s32[2]{0:T(128)}, u32[]{:S(2)}) copy-start(s32[2]{0:T(128)} %get-tuple-element.48.refs_0_) | copy-start | bytes 28
  77.2 23.0 %collective-permute-start.3 = (bf16[2,128,1152]{2,1,0:T(8,128)(2,1)}, bf16[2,128,1152]{2,1,0:T(8,128)(2,1)S(1)}, u32[]{:S(2)}, u32[]{:S(2)}) collective-permute-start(bf16[2,128,1152]{2,1,0:T(8,128)(2,1)} %get-tuple-element.63), channel_id=1, source_target_pairs={{0,1},{1,2},{2,3},{3,4},{4,5},{5,6},{6,7},{7,0},{8,9},{9,10},{10,1... | collective-permute-start | bytes 1769480 | tf_op jit(solution)/shard_map/ppermute | solution.py:280
  78.8 21.4 %collective-permute-start.4 = (bf16[2,128,1152]{2,1,0:T(8,128)(2,1)}, bf16[2,128,1152]{2,1,0:T(8,128)(2,1)S(1)}, u32[]{:S(2)}, u32[]{:S(2)}) collective-permute-start(bf16[2,128,1152]{2,1,0:T(8,128)(2,1)} %get-tuple-element.64), channel_id=1, source_target_pairs={{0,7},{1,0},{2,1},{3,2},{4,3},{5,4},{6,5},{7,6},{8,15},{9,8},{10,9... | collective-permute-start | bytes 1769480 | tf_op jit(solution)/shard_map/ppermute | solution.py:280
  85.7 34.6 %collective-permute-start = (bf16[2,128,1152]{2,1,0:T(8,128)(2,1)}, bf16[2,128,1152]{2,1,0:T(8,128)(2,1)S(1)}, u32[]{:S(2)}, u32[]{:S(2)}) collective-permute-start(bf16[2,128,1152]{2,1,0:T(8,128)(2,1)} %get-tuple-element.60), channel_id=1, source_target_pairs={{0,8},{1,9},{2,10},{3,11},{4,12},{5,13},{6,14},{7,15},{8,0},{9,1},... | collective-permute-start | bytes 1769480 | tf_op jit(solution)/shard_map/ppermute | solution.py:284
  89.7 24.1 %collective-permute-start.1 = (bf16[2,128,1152]{2,1,0:T(8,128)(2,1)}, bf16[2,128,1152]{2,1,0:T(8,128)(2,1)}, u32[]{:S(2)}, u32[]{:S(2)}) collective-permute-start(bf16[2,128,1152]{2,1,0:T(8,128)(2,1)} %get-tuple-element.61), channel_id=1, source_target_pairs={{0,1},{1,2},{2,3},{3,4},{4,5},{5,6},{6,7},{7,0},{8,9},{9,10},{10,1... | collective-permute-start | bytes 1769480 | tf_op jit(solution)/shard_map/ppermute | solution.py:280
  89.7 24.1 %collective-permute-start.2 = (bf16[2,128,1152]{2,1,0:T(8,128)(2,1)}, bf16[2,128,1152]{2,1,0:T(8,128)(2,1)}, u32[]{:S(2)}, u32[]{:S(2)}) collective-permute-start(bf16[2,128,1152]{2,1,0:T(8,128)(2,1)} %get-tuple-element.62), channel_id=1, source_target_pairs={{0,7},{1,0},{2,1},{3,2},{4,3},{5,4},{6,5},{7,6},{8,15},{9,8},{10,9... | collective-permute-start | bytes 1769480 | tf_op jit(solution)/shard_map/ppermute | solution.py:280
  103.7 19.8 %collective-permute-start.5 = (bf16[2,128,1152]{2,1,0:T(8,128)(2,1)}, bf16[2,128,1152]{2,1,0:T(8,128)(2,1)S(1)}, u32[]{:S(2)}, u32[]{:S(2)}) collective-permute-start(bf16[2,128,1152]{2,1,0:T(8,128)(2,1)} %get-tuple-element.69), channel_id=1, source_target_pairs={{0,1},{1,2},{2,3},{3,4},{4,5},{5,6},{6,7},{7,0},{8,9},{9,10},{10,1... | collective-permute-start | bytes 1769480 | tf_op jit(solution)/shard_map/ppermute | solution.py:280
  103.7 19.8 %collective-permute-start.6 = (bf16[2,128,1152]{2,1,0:T(8,128)(2,1)}, bf16[2,128,1152]{2,1,0:T(8,128)(2,1)}, u32[]{:S(2)}, u32[]{:S(2)}) collective-permute-start(bf16[2,128,1152]{2,1,0:T(8,128)(2,1)} %get-tuple-element.70), channel_id=1, source_target_pairs={{0,7},{1,0},{2,1},{3,2},{4,3},{5,4},{6,5},{7,6},{8,15},{9,8},{10,9... | collective-permute-start | bytes 1769480 | tf_op jit(solution)/shard_map/ppermute | solution.py:280
  106.4 66.3 %all-to-all-start.1 = ((bf16[16,32,2176]{2,1,0:T(8,128)(2,1)}), bf16[16,32,2176]{2,1,0:T(8,128)(2,1)}, u32[]{:S(2)}, u32[]{:S(2)}) async-start(bf16[16,32,2176]{2,1,0:T(8,128)(2,1)} %bitcast.66), calls=%async_computation.1 | async-start | bytes 4456448 | tf_op jit(solution)/shard_map/all_to_all | solution.py:440
  117.7 16.8 %collective-permute-start.9 = (bf16[2,128,1152]{2,1,0:T(8,128)(2,1)}, bf16[2,128,1152]{2,1,0:T(8,128)(2,1)S(1)}, u32[]{:S(2)}, u32[]{:S(2)}) collective-permute-start(bf16[2,128,1152]{2,1,0:T(8,128)(2,1)} %get-tuple-element.74), channel_id=1, source_target_pairs={{0,1},{1,2},{2,3},{3,4},{4,5},{5,6},{6,7},{7,0},{8,9},{9,10},{10,1... | collective-permute-start | bytes 1769480 | tf_op jit(solution)/shard_map/ppermute | solution.py:280
  117.7 16.8 %collective-permute-start.10 = (bf16[2,128,1152]{2,1,0:T(8,128)(2,1)}, bf16[2,128,1152]{2,1,0:T(8,128)(2,1)S(1)}, u32[]{:S(2)}, u32[]{:S(2)}) collective-permute-start(bf16[2,128,1152]{2,1,0:T(8,128)(2,1)} %get-tuple-element.75), channel_id=1, source_target_pairs={{0,7},{1,0},{2,1},{3,2},{4,3},{5,4},{6,5},{7,6},{8,15},{9,8},{10,9... | collective-permute-start | bytes 1769480 | tf_op jit(solution)/shard_map/ppermute | solution.py:280
  122.5 1.0 copy-start.1
  127.2 19.8 %collective-permute-start.7 = (bf16[2,128,1152]{2,1,0:T(8,128)(2,1)}, bf16[2,128,1152]{2,1,0:T(8,128)(2,1)S(1)}, u32[]{:S(2)}, u32[]{:S(2)}) collective-permute-start(bf16[2,128,1152]{2,1,0:T(8,128)(2,1)} %get-tuple-element.72), channel_id=1, source_target_pairs={{0,1},{1,2},{2,3},{3,4},{4,5},{5,6},{6,7},{7,0},{8,9},{9,10},{10,1... | collective-permute-start | bytes 1769480 | tf_op jit(solution)/shard_map/ppermute | solution.py:280
  127.2 19.8 %collective-permute-start.8 = (bf16[2,128,1152]{2,1,0:T(8,128)(2,1)}, bf16[2,128,1152]{2,1,0:T(8,128)(2,1)S(1)}, u32[]{:S(2)}, u32[]{:S(2)}) collective-permute-start(bf16[2,128,1152]{2,1,0:T(8,128)(2,1)} %get-tuple-element.73), channel_id=1, source_target_pairs={{0,7},{1,0},{2,1},{3,2},{4,3},{5,4},{6,5},{7,6},{8,15},{9,8},{10,9... | collective-permute-start | bytes 1769480 | tf_op jit(solution)/shard_map/ppermute | solution.py:280
  137.9 18.0 %collective-permute-start.12 = (bf16[2,128,1152]{2,1,0:T(8,128)(2,1)}, bf16[2,128,1152]{2,1,0:T(8,128)(2,1)S(1)}, u32[]{:S(2)}, u32[]{:S(2)}) collective-permute-start(bf16[2,128,1152]{2,1,0:T(8,128)(2,1)} %get-tuple-element.81), channel_id=1, source_target_pairs={{0,8},{1,9},{2,10},{3,11},{4,12},{5,13},{6,14},{7,15},{8,0},{9,1},... | collective-permute-start | bytes 1769480 | tf_op jit(solution)/shard_map/ppermute | solution.py:284
  150.6 18.0 %collective-permute-start.11 = (bf16[2,128,1152]{2,1,0:T(8,128)(2,1)}, bf16[2,128,1152]{2,1,0:T(8,128)(2,1)S(1)}, u32[]{:S(2)}, u32[]{:S(2)}) collective-permute-start(bf16[2,128,1152]{2,1,0:T(8,128)(2,1)} %get-tuple-element.79), channel_id=1, source_target_pairs={{0,8},{1,9},{2,10},{3,11},{4,12},{5,13},{6,14},{7,15},{8,0},{9,1},... | collective-permute-start | bytes 1769480 | tf_op jit(solution)/shard_map/ppermute | solution.py:284
  157.4 18.3 %collective-permute-start.15 = (bf16[1,128,1152]{2,1,0:T(8,128)(2,1)}, bf16[1,128,1152]{2,1,0:T(8,128)(2,1)S(1)}, u32[]{:S(2)}, u32[]{:S(2)}) collective-permute-start(bf16[1,128,1152]{2,1,0:T(8,128)(2,1)} %get-tuple-element.86), channel_id=1, source_target_pairs={{0,1},{1,2},{2,3},{3,4},{4,5},{5,6},{6,7},{7,0},{8,9},{9,10},{10,1... | collective-permute-start | bytes 884744 | tf_op jit(solution)/shard_map/ppermute | solution.py:280
  157.4 18.3 %collective-permute-start.16 = (bf16[1,128,1152]{2,1,0:T(8,128)(2,1)}, bf16[1,128,1152]{2,1,0:T(8,128)(2,1)S(1)}, u32[]{:S(2)}, u32[]{:S(2)}) collective-permute-start(bf16[1,128,1152]{2,1,0:T(8,128)(2,1)} %get-tuple-element.87), channel_id=1, source_target_pairs={{0,7},{1,0},{2,1},{3,2},{4,3},{5,4},{6,5},{7,6},{8,15},{9,8},{10,9... | collective-permute-start | bytes 884744 | tf_op jit(solution)/shard_map/ppermute | solution.py:280
  168.6 4.1 %copy-start.4 = (bf16[128,2]{0,1:T(2,128)(2,1)S(1)}, bf16[128,2]{0,1:T(2,128)(2,1)}, u32[]{:S(2)}) copy-start(bf16[128,2]{0,1:T(2,128)(2,1)} %param.9) | copy-start | bytes 1540
  168.6 4.1 %copy-start.5 = (s32[2,128]{1,0:T(2,128)S(1)}, s32[2,128]{1,0:T(2,128)}, u32[]{:S(2)}) copy-start(s32[2,128]{1,0:T(2,128)} %get-tuple-element.47.target_ref) | copy-start | bytes 3076
  170.0 8.5 %copy-start.2 = (f32[2,128,1152]{2,1,0:T(8,128)S(1)}, f32[2,128,1152]{2,1,0:T(8,128)}, u32[]{:S(2)}) copy-start(f32[2,128,1152]{2,1,0:T(8,128)} %copy-done.1) | copy-start | bytes 3538948
  170.0 8.5 %collective-permute-start.13 = (bf16[1,128,1152]{2,1,0:T(8,128)(2,1)}, bf16[1,128,1152]{2,1,0:T(8,128)(2,1)S(1)}, u32[]{:S(2)}, u32[]{:S(2)}) collective-permute-start(bf16[1,128,1152]{2,1,0:T(8,128)(2,1)} %get-tuple-element.84), channel_id=1, source_target_pairs={{0,1},{1,2},{2,3},{3,4},{4,5},{5,6},{6,7},{7,0},{8,9},{9,10},{10,1... | collective-permute-start | bytes 884744 | tf_op jit(solution)/shard_map/ppermute | solution.py:280
  170.0 8.5 %collective-permute-start.14 = (bf16[1,128,1152]{2,1,0:T(8,128)(2,1)}, bf16[1,128,1152]{2,1,0:T(8,128)(2,1)S(1)}, u32[]{:S(2)}, u32[]{:S(2)}) collective-permute-start(bf16[1,128,1152]{2,1,0:T(8,128)(2,1)} %get-tuple-element.85), channel_id=1, source_target_pairs={{0,7},{1,0},{2,1},{3,2},{4,3},{5,4},{6,5},{7,6},{8,15},{9,8},{10,9... | collective-permute-start | bytes 884744 | tf_op jit(solution)/shard_map/ppermute | solution.py:280

commit v4 on v3

--- a/solution.py
+++ b/solution.py
@@ -401,6 +401,10 @@
     x_pair = onward(sent)
     sent, token = hop("hop_y2", far - 2, False, y_pair, (token,))
     y_pair = onward(sent)
+    sent, token = hop("hop_x2", far - 2, True, x_pair, (token, own_other))
+    x_pair = onward(sent)
+    (y_kept, sent), token = split_hop("hop_y1", far - 3, False, y_pair, (token,))
+    y_other = swap(sent)
     (base,), token = some_terms(
         "own",
         [
@@ -414,10 +418,6 @@
         ],
         (token,),
     )
-    sent, token = hop("hop_x2", far - 2, True, x_pair, (token,))
-    x_pair = onward(sent)
-    (y_kept, sent), token = split_hop("hop_y1", far - 3, False, y_pair, (token,))
-    y_other = swap(sent)
     (x_kept, sent), token = split_hop("hop_x1", far - 3, True, x_pair, (token,))
     x_other = swap(sent)
     sent, token = joined("joined_y", y_kept, y_other, (token,))

time: 182 us -> 182 us (level)
  transfers between devices with their start and end apart: 18 -> 18, of which waited for: 5 -> 6; matrix products, arithmetic and copies ran while one was open for 0% -> 0% of each run, Pallas kernels for 22% -> 22%
where the time goes in v4:
time: 182 us; the launch traced here: 180 us
  blocking collectives  59.3 us (33%)
  Pallas kernels  59.2 us (33%)
  starting transfers between devices  30 us (16%)
  waiting for transfers between devices  29.8 us (16%)
    all_to_all x1, blocking collectives, shards(): lax.all_to_all(send.reshape(experts, capacity, 2 * width), 'blk', split_a...  59.3 us
    pallas_call x13, Pallas kernels, call(): pl.pallas_call(body, grid_spec=pltpu.PrefetchScalarGridSpec(num_scalar_pr...  42.5 us
    ppermute x14, starting transfers between devices, permute(): return lax.ppermute(array, 'rep', pairs)  21.6 us
    ppermute x14, waiting for transfers between devices, permute(): return lax.ppermute(array, 'rep', pairs)  16.2 us
    ppermute x3, waiting for transfers between devices, swap(): return lax.ppermute(array, 'rep', pairs)  13.7 us
    pallas_call x1, Pallas kernels, shards(): pl.pallas_call(rows_kernel, grid=(steps,), in_specs=[whole((slots, 2 * wi...  9.05 us
    all_to_all x1, starting transfers between devices, shards(): lax.all_to_all(back.reshape(experts, capacity, width + LANES), 'blk', spl...  7.36 us
    pallas_call x1, Pallas kernels, shards(): pl.pallas_call(functools.partial(dispatch_kernel, experts=experts, ring=r...  4.69 us
  transfers between devices with their start and end apart: 18, of which 6 were waited for; matrix products, arithmetic and copies ran while one was open for 0% of the time, Pallas kernels for 22%

profile of v4, /device:TPU:1, one launch (start us, length us, event | category | flops | bytes accessed | tf_op | source)
XLA Modules:
  0.0 180.1 jit_solution(10211487628551348657)
XLA Ops:
  0.6 4.7 %dispatch.1 = (bf16[512,4096]{1,0:T(8,128)(2,1)}, s32[2,128]{1,0:T(2,128)}, s32[2]{0:T(128)}) custom-call(s32[2,128]{1,0:T(2,128)} %bitcast.67, bf16[2,128]{1,0:T(2,128)(2,1)} %bitcast.10, bf16[128,2048]{1,0:T(8,128)(2,1)} %tokens_ref.1, bf16[128,2048]{1,0:T(8,128)(2,1)} %grads_ref.1), custom_call_target="tpu_custom_call" | custom-call | tf_op jit(solution)/shard_map/dispatch/pallas_call | solution.py:201
  5.3 0.0 copy-start
  5.3 59.3 %all_to_all.10 = bf16[16,32,4096]{2,1,0:T(8,128)(2,1)} all-to-all(bf16[16,32,4096]{2,1,0:T(8,128)(2,1)} %bitcast.65), channel_id=1, replica_groups=mesh['blk'=16,'rep'=16] {'blk'}, dimensions={0} | all-to-all | bytes 8388608 | tf_op jit(solution)/shard_map/all_to_all | solution.py:217
  64.6 0.0 copy-done
  64.6 0.0 copy-start.3
  64.6 9.0 %rows.1 = (bf16[512,768]{1,0:T(8,128)(2,1)S(1)}, bf16[512,768]{1,0:T(8,128)(2,1)S(1)}, bf16[512,768]{1,0:T(8,128)(2,1)S(1)}, f32[512,128]{1,0:T(8,128)S(1)}) custom-call(bf16[512,4096]{1,0:T(8,128)(2,1)} %bitcast.12, bf16[2048,1536]{1,0:T(8,128)(2,1)} %bitcast.61, bf16[2048,1536]{1,0:T(8,128)(2,1)} %bitcast.62, bf16[2048,768]{1,0:T(8,128)(2,1)S(1)} %bitcast.9), custom_call_target="tpu_custom_call" | custom-call | tf_op jit(solution)/shard_map/rows/pallas_call | solution.py:223
  73.7 0.0 copy-done.3
  73.7 3.5 %first_x.1 = (bf16[2,128,1152]{2,1,0:T(8,128)(2,1)}, bf16[2,128,1152]{2,1,0:T(8,128)(2,1)}, f32[8,128]{1,0:T(8,128)S(1)}) custom-call(s32[2]{0:T(128)S(1)} %copy-done.3, bf16[512,768]{1,0:T(8,128)(2,1)S(1)} %get-tuple-element.53.refs_1_, bf16[512,768]{1,0:T(8,128)(2,1)S(1)} %get-tuple-element.50.refs_2_.refs_1_, ...), custom_call_target="tpu_custom_call" | custom-call | flops 1 | bytes 1 | tf_op jit(solution)/shard_map/first_x/pallas_call | solution.py:256
  77.2 1.6 collective-permute-start.3
  78.8 3.9 %collective-permute-start.4 = (bf16[2,128,1152]{2,1,0:T(8,128)(2,1)}, bf16[2,128,1152]{2,1,0:T(8,128)(2,1)S(1)}, u32[]{:S(2)}, u32[]{:S(2)}) collective-permute-start(bf16[2,128,1152]{2,1,0:T(8,128)(2,1)} %get-tuple-element.64), channel_id=1, source_target_pairs={{0,7},{1,0},{2,1},{3,2},{4,3},{5,4},{6,5},{7,6},{8,15},{9,8},{10,9... | collective-permute-start | bytes 1769480 | tf_op jit(solution)/shard_map/ppermute | solution.py:280
  82.8 3.0 %own_theirs.1 = (bf16[2,128,1152]{2,1,0:T(8,128)(2,1)}, f32[8,128]{1,0:T(8,128)S(1)}) custom-call(s32[2]{0:T(128)S(1)} %copy-done.3, bf16[512,768]{1,0:T(8,128)(2,1)S(1)} %get-tuple-element.53.refs_1_, bf16[512,768]{1,0:T(8,128)(2,1)S(1)} %get-tuple-element.50.refs_2_.refs_1_, bf16[512,768]{1,0:T(8,128)(2,1)S(1)} %get-tuple-element.51.refs_3_.refs_2_, ...), custom_call_target="tpu_custom_call" | custom-call | flops 1 | bytes 1 | tf_op jit(solution)/shard_map/own_theirs/pallas_call | solution.py:256
  85.7 0.4 collective-permute-start
  86.1 3.6 %first_y.1 = (bf16[2,128,1152]{2,1,0:T(8,128)(2,1)}, bf16[2,128,1152]{2,1,0:T(8,128)(2,1)}, f32[8,128]{1,0:T(8,128)S(1)}) custom-call(s32[2]{0:T(128)S(1)} %copy-done.3, bf16[512,768]{1,0:T(8,128)(2,1)S(1)} %get-tuple-element.53.refs_1_, bf16[512,768]{1,0:T(8,128)(2,1)S(1)} %get-tuple-element.50.refs_2_.refs_1_, ...), custom_call_target="tpu_custom_call" | custom-call | flops 1 | bytes 1 | tf_op jit(solution)/shard_map/first_y/pallas_call | solution.py:256
  89.7 0.0 collective-permute-start.1
  89.7 2.7 %collective-permute-start.2 = (bf16[2,128,1152]{2,1,0:T(8,128)(2,1)}, bf16[2,128,1152]{2,1,0:T(8,128)(2,1)}, u32[]{:S(2)}, u32[]{:S(2)}) collective-permute-start(bf16[2,128,1152]{2,1,0:T(8,128)(2,1)} %get-tuple-element.62), channel_id=1, source_target_pairs={{0,7},{1,0},{2,1},{3,2},{4,3},{5,4},{6,5},{7,6},{8,15},{9,8},{10,9... | collective-permute-start | bytes 1769480 | tf_op jit(solution)/shard_map/ppermute | solution.py:280
  92.4 7.8 %row_grads.1 = (bf16[512,2176]{1,0:T(8,128)(2,1)}, f32[8,128]{1,0:T(8,128)S(1)}) custom-call(s32[2]{0:T(128)S(1)} %copy-done.3, bf16[512,768]{1,0:T(8,128)(2,1)S(1)} %get-tuple-element.50.refs_2_.refs_1_, bf16[512,768]{1,0:T(8,128)(2,1)S(1)} %get-tuple-element.51.refs_3_.refs_2_, bf16[2048,1536]{1,0:T(8,128)(2,1)} %bitcast.63, bf16[2048,1536]{1,0:T(8,128)(2,1)} %bitcast.64, ...), custom_call_target="tpu_custom_call" | custom-call | flops 1 | bytes 1 | tf_op jit(solution)/shard_map/row_grads/pallas_call | solution.py:256
  100.2 0.0 collective-permute-done.3.refs_5_.refs_7_
  100.2 0.0 collective-permute-done.4.refs_10_.refs_13_
  100.2 3.5 %hop_x3.1 = (bf16[2,128,1152]{2,1,0:T(8,128)(2,1)}, bf16[2,128,1152]{2,1,0:T(8,128)(2,1)}, f32[8,128]{1,0:T(8,128)S(1)}) custom-call(s32[2]{0:T(128)S(1)} %copy-done.3, bf16[512,768]{1,0:T(8,128)(2,1)S(1)} %get-tuple-element.53.refs_1_, bf16[512,768]{1,0:T(8,128)(2,1)S(1)} %get-tuple-element.50.refs_2_.refs_1_, ...), custom_call_target="tpu_custom_call" | custom-call | flops 1 | bytes 1 | tf_op jit(solution)/shard_map/hop_x3/pallas_call | solution.py:256
  103.7 0.0 collective-permute-start.7
  103.7 2.7 %collective-permute-start.8 = (bf16[2,128,1152]{2,1,0:T(8,128)(2,1)}, bf16[2,128,1152]{2,1,0:T(8,128)(2,1)}, u32[]{:S(2)}, u32[]{:S(2)}) collective-permute-start(bf16[2,128,1152]{2,1,0:T(8,128)(2,1)} %get-tuple-element.70), channel_id=1, source_target_pairs={{0,7},{1,0},{2,1},{3,2},{4,3},{5,4},{6,5},{7,6},{8,15},{9,8},{10,9... | collective-permute-start | bytes 1769480 | tf_op jit(solution)/shard_map/ppermute | solution.py:280
  106.4 7.4 %all-to-all-start.1 = ((bf16[16,32,2176]{2,1,0:T(8,128)(2,1)}), bf16[16,32,2176]{2,1,0:T(8,128)(2,1)}, u32[]{:S(2)}, u32[]{:S(2)}) async-start(bf16[16,32,2176]{2,1,0:T(8,128)(2,1)} %bitcast.66), calls=%async_computation.1 | async-start | bytes 4456448 | tf_op jit(solution)/shard_map/all_to_all | solution.py:440
  113.8 0.0 collective-permute-done.1.refs_6_.refs_9_
  113.8 0.0 collective-permute-done.2.refs_11_.refs_13_
  113.8 3.7 %hop_y2.1 = (bf16[2,128,1152]{2,1,0:T(8,128)(2,1)}, bf16[2,128,1152]{2,1,0:T(8,128)(2,1)}, f32[8,128]{1,0:T(8,128)S(1)}) custom-call(s32[2]{0:T(128)S(1)} %copy-done.3, bf16[512,768]{1,0:T(8,128)(2,1)S(1)} %get-tuple-element.53.refs_1_, bf16[512,768]{1,0:T(8,128)(2,1)S(1)} %get-tuple-element.50.refs_2_.refs_1_, ...), custom_call_target="tpu_custom_call" | custom-call | flops 1 | bytes 1 | tf_op jit(solution)/shard_map/hop_y2/pallas_call | solution.py:256
  117.5 0.0 collective-permute-start.5
  117.5 2.7 %collective-permute-start.6 = (bf16[2,128,1152]{2,1,0:T(8,128)(2,1)}, bf16[2,128,1152]{2,1,0:T(8,128)(2,1)S(1)}, u32[]{:S(2)}, u32[]{:S(2)}) collective-permute-start(bf16[2,128,1152]{2,1,0:T(8,128)(2,1)} %get-tuple-element.68), channel_id=1, source_target_pairs={{0,7},{1,0},{2,1},{3,2},{4,3},{5,4},{6,5},{7,6},{8,15},{9,8},{10,9... | collective-permute-start | bytes 1769480 | tf_op jit(solution)/shard_map/ppermute | solution.py:280
  120.2 0.0 collective-permute-done.refs_15_.refs_5_.refs_8_
  120.2 0.5 collective-permute-done.7.refs_5_.refs_7_
  120.7 0.0 collective-permute-done.8.refs_10_.refs_13_
  120.7 3.8 %hop_x2.1 = (bf16[2,128,1152]{2,1,0:T(8,128)(2,1)}, bf16[2,128,1152]{2,1,0:T(8,128)(2,1)}, f32[8,128]{1,0:T(8,128)S(1)}) custom-call(s32[2]{0:T(128)S(1)} %copy-done.3, bf16[512,768]{1,0:T(8,128)(2,1)S(1)} %get-tuple-element.53.refs_1_, bf16[512,768]{1,0:T(8,128)(2,1)S(1)} %get-tuple-element.50.refs_2_.refs_1_, ...), custom_call_target="tpu_custom_call" | custom-call | flops 1 | bytes 1 | tf_op jit(solution)/shard_map/hop_x2/pallas_call | solution.py:256
  124.4 0.0 collective-permute-start.9
  124.5 2.7 %collective-permute-start.10 = (bf16[2,128,1152]{2,1,0:T(8,128)(2,1)}, bf16[2,128,1152]{2,1,0:T(8,128)(2,1)S(1)}, u32[]{:S(2)}, u32[]{:S(2)}) collective-permute-start(bf16[2,128,1152]{2,1,0:T(8,128)(2,1)} %get-tuple-element.76), channel_id=1, source_target_pairs={{0,7},{1,0},{2,1},{3,2},{4,3},{5,4},{6,5},{7,6},{8,15},{9,8},{10,9... | collective-permute-start | bytes 1769480 | tf_op jit(solution)/shard_map/ppermute | solution.py:280
  127.1 7.2 %collective-permute-done.5.refs_6_.refs_11_ = bf16[2,128,1152]{2,1,0:T(8,128)(2,1)S(1)} collective-permute-done((bf16[2,128,1152]{2,1,0:T(8,128)(2,1)}, bf16[2,128,1152]{2,1,0:T(8,128)(2,1)S(1)}, u32[]{:S(2)}, u32[]{:S(2)}) %collective-permute-start.5) | collective-permute-done | bytes 589856 | tf_op jit(solution)/shard_map/ppermute | solution.py:280
  134.3 0.0 collective-permute-done.6.refs_8_.refs_13_
  134.3 3.5 %hop_y1.1 = (f32[2,128,1152]{2,1,0:T(8,128)S(1)}, bf16[2,128,1152]{2,1,0:T(8,128)(2,1)}, f32[8,128]{1,0:T(8,128)S(1)}) custom-call(s32[2]{0:T(128)S(1)} %copy-done.3, bf16[512,768]{1,0:T(8,128)(2,1)S(1)} %get-tuple-element.53.refs_1_, bf16[512,768]{1,0:T(8,128)(2,1)S(1)} %get-tuple-element.50.refs_2_.refs_1_, ...), custom_call_target="tpu_custom_call" | custom-call | flops 1 | bytes 1 | tf_op jit(solution)/shard_map/hop_y1/pallas_call | solution.py:256
  137.8 0.3 collective-permute-start.12
  138.1 2.1 %own.1 = (f32[2,128,1152]{2,1,0:T(8,128)S(1)}, f32[8,128]{1,0:T(8,128)S(1)}) custom-call(s32[2]{0:T(128)S(1)} %copy-done.3, bf16[512,768]{1,0:T(8,128)(2,1)S(1)} %get-tuple-element.53.refs_1_, bf16[512,768]{1,0:T(8,128)(2,1)S(1)} %get-tuple-element.50.refs_2_.refs_1_, bf16[512,768]{1,0:T(8,128)(2,1)S(1)} %get-tuple-element.51.refs_3_.refs_2_, ...), custom_call_target="tpu_custom_call" | custom-call | flops 1 | bytes 1 | tf_op jit(solution)/shard_map/own/pallas_call | solution.py:256
  140.3 0.0 copy-start.1
  140.3 1.0 copy-done.1
  141.3 5.7 %collective-permute-done.9.refs_5_.refs_10_ = bf16[2,128,1152]{2,1,0:T(8,128)(2,1)S(1)} collective-permute-done((bf16[2,128,1152]{2,1,0:T(8,128)(2,1)}, bf16[2,128,1152]{2,1,0:T(8,128)(2,1)S(1)}, u32[]{:S(2)}, u32[]{:S(2)}) %collective-permute-start.9) | collective-permute-done | bytes 589856 | tf_op jit(solution)/shard_map/ppermute | solution.py:280
  147.0 0.0 collective-permute-done.10.refs_8_.refs_13_
  147.0 3.5 %hop_x1.1 = (f32[2,128,1152]{2,1,0:T(8,128)S(1)}, bf16[2,128,1152]{2,1,0:T(8,128)(2,1)}, f32[8,128]{1,0:T(8,128)S(1)}) custom-call(s32[2]{0:T(128)S(1)} %copy-done.3, bf16[512,768]{1,0:T(8,128)(2,1)S(1)} %get-tuple-element.53.refs_1_, bf16[512,768]{1,0:T(8,128)(2,1)S(1)} %get-tuple-element.50.refs_2_.refs_1_, ...), custom_call_target="tpu_custom_call" | custom-call | flops 1 | bytes 1 | tf_op jit(solution)/shard_map/hop_x1/pallas_call | solution.py:256
  150.5 0.3 collective-permute-start.11
  150.8 5.1 %collective-permute-done.12.refs_2_ = bf16[2,128,1152]{2,1,0:T(8,128)(2,1)S(1)} collective-permute-done((bf16[2,128,1152]{2,1,0:T(8,128)(2,1)}, bf16[2,128,1152]{2,1,0:T(8,128)(2,1)S(1)}, u32[]{:S(2)}, u32[]{:S(2)}) %collective-permute-start.12) | collective-permute-done | bytes 589856 | tf_op jit(solution)/shard_map/ppermute | solution.py:284
  155.9 1.4 joined_y.1
  157.3 0.0 collective-permute-start.15
  157.3 2.7 %collective-permute-start.16 = (bf16[1,128,1152]{2,1,0:T(8,128)(2,1)}, bf16[1,128,1152]{2,1,0:T(8,128)(2,1)S(1)}, u32[]{:S(2)}, u32[]{:S(2)}) collective-permute-start(bf16[1,128,1152]{2,1,0:T(8,128)(2,1)} %get-tuple-element.87), channel_id=1, source_target_pairs={{0,7},{1,0},{2,1},{3,2},{4,3},{5,4},{6,5},{7,6},{8,15},{9,8},{10,9... | collective-permute-start | bytes 884744 | tf_op jit(solution)/shard_map/ppermute | solution.py:280
  160.0 8.5 %collective-permute-done.11.refs_2_ = bf16[2,128,1152]{2,1,0:T(8,128)(2,1)S(1)} collective-permute-done((bf16[2,128,1152]{2,1,0:T(8,128)(2,1)}, bf16[2,128,1152]{2,1,0:T(8,128)(2,1)S(1)}, u32[]{:S(2)}, u32[]{:S(2)}) %collective-permute-start.11) | collective-permute-done | bytes 589856 | tf_op jit(solution)/shard_map/ppermute | solution.py:284
  168.5 0.0 copy-start.4
  168.5 0.0 copy-start.5
  168.5 1.4 joined_x.1
  170.0 0.0 collective-permute-start.13
  170.0 2.7 %collective-permute-start.14 = (bf16[1,128,1152]{2,1,0:T(8,128)(2,1)}, bf16[1,128,1152]{2,1,0:T(8,128)(2,1)S(1)}, u32[]{:S(2)}, u32[]{:S(2)}) collective-permute-start(bf16[1,128,1152]{2,1,0:T(8,128)(2,1)} %get-tuple-element.85), channel_id=1, source_target_pairs={{0,7},{1,0},{2,1},{3,2},{4,3},{5,4},{6,5},{7,6},{8,15},{9,8},{10,9... | collective-permute-start | bytes 884744 | tf_op jit(solution)/shard_map/ppermute | solution.py:280
  172.6 0.0 all-to-all-done.1
  172.6 0.0 copy-done.4
  172.7 0.0 copy-done.5
  172.7 2.9 %home.1 = (bf16[128,2048]{1,0:T(8,128)(2,1)}, bf16[2,128]{1,0:T(2,128)(2,1)}) custom-call(s32[2,128]{1,0:T(2,128)S(1)} %copy-done.5, bf16[2,128]{1,0:T(2,128)(2,1)S(1)} %bitcast.11, bf16[512,2176]{1,0:T(8,128)(2,1)} %bitcast.7.back_ref), custom_call_target="tpu_custom_call" | custom-call | tf_op jit(solution)/shard_map/home/pallas_call | solution.py:444
  175.6 0.0 collective-permute-done.15.refs_4_
  175.6 0.0 collective-permute-done.16.refs_5_
  175.6 2.8 %collective-permute-done.13.refs_2_ = bf16[1,128,1152]{2,1,0:T(8,128)(2,1)S(1)} collective-permute-done((bf16[1,128,1152]{2,1,0:T(8,128)(2,1)}, bf16[1,128,1152]{2,1,0:T(8,128)(2,1)S(1)}, u32[]{:S(2)}, u32[]{:S(2)}) %collective-permute-start.13) | collective-permute-done | bytes 294944 | tf_op jit(solution)/shard_map/ppermute | solution.py:280
  178.4 0.0 collective-permute-done.14.refs_3_
  178.4 0.0 copy-done.2
  178.4 1.7 total.1
  (1 shorter events, 0.0 us)
Async XLA Ops:
  5.3 59.3 %copy-start = (bf16[1,2048,768]{2,1,0:T(8,128)(2,1)S(1)}, bf16[1,2048,768]{2,1,0:T(8,128)(2,1)}, u32[]{:S(2)}) copy-start(bf16[1,2048,768]{2,1,0:T(8,128)(2,1)} %param.11) | copy-start | bytes 9437188
  64.6 9.1 %copy-start.3 = (s32[2]{0:T(128)S(1)}, s32[2]{0:T(128)}, u32[]{:S(2)}) copy-start(s32[2]{0:T(128)} %get-tuple-element.48.refs_0_) | copy-start | bytes 28
  77.2 23.0 %collective-permute-start.3 = (bf16[2,128,1152]{2,1,0:T(8,128)(2,1)}, bf16[2,128,1152]{2,1,0:T(8,128)(2,1)S(1)}, u32[]{:S(2)}, u32[]{:S(2)}) collective-permute-start(bf16[2,128,1152]{2,1,0:T(8,128)(2,1)} %get-tuple-element.63), channel_id=1, source_target_pairs={{0,1},{1,2},{2,3},{3,4},{4,5},{5,6},{6,7},{7,0},{8,9},{9,10},{10,1... | collective-permute-start | bytes 1769480 | tf_op jit(solution)/shard_map/ppermute | solution.py:280
  78.8 21.4 %collective-permute-start.4 = (bf16[2,128,1152]{2,1,0:T(8,128)(2,1)}, bf16[2,128,1152]{2,1,0:T(8,128)(2,1)S(1)}, u32[]{:S(2)}, u32[]{:S(2)}) collective-permute-start(bf16[2,128,1152]{2,1,0:T(8,128)(2,1)} %get-tuple-element.64), channel_id=1, source_target_pairs={{0,7},{1,0},{2,1},{3,2},{4,3},{5,4},{6,5},{7,6},{8,15},{9,8},{10,9... | collective-permute-start | bytes 1769480 | tf_op jit(solution)/shard_map/ppermute | solution.py:280
  85.7 34.4 %collective-permute-start = (bf16[2,128,1152]{2,1,0:T(8,128)(2,1)}, bf16[2,128,1152]{2,1,0:T(8,128)(2,1)S(1)}, u32[]{:S(2)}, u32[]{:S(2)}) collective-permute-start(bf16[2,128,1152]{2,1,0:T(8,128)(2,1)} %get-tuple-element.60), channel_id=1, source_target_pairs={{0,8},{1,9},{2,10},{3,11},{4,12},{5,13},{6,14},{7,15},{8,0},{9,1},... | collective-permute-start | bytes 1769480 | tf_op jit(solution)/shard_map/ppermute | solution.py:284
  89.7 24.1 %collective-permute-start.1 = (bf16[2,128,1152]{2,1,0:T(8,128)(2,1)}, bf16[2,128,1152]{2,1,0:T(8,128)(2,1)S(1)}, u32[]{:S(2)}, u32[]{:S(2)}) collective-permute-start(bf16[2,128,1152]{2,1,0:T(8,128)(2,1)} %get-tuple-element.61), channel_id=1, source_target_pairs={{0,1},{1,2},{2,3},{3,4},{4,5},{5,6},{6,7},{7,0},{8,9},{9,10},{10,1... | collective-permute-start | bytes 1769480 | tf_op jit(solution)/shard_map/ppermute | solution.py:280
  89.7 24.1 %collective-permute-start.2 = (bf16[2,128,1152]{2,1,0:T(8,128)(2,1)}, bf16[2,128,1152]{2,1,0:T(8,128)(2,1)}, u32[]{:S(2)}, u32[]{:S(2)}) collective-permute-start(bf16[2,128,1152]{2,1,0:T(8,128)(2,1)} %get-tuple-element.62), channel_id=1, source_target_pairs={{0,7},{1,0},{2,1},{3,2},{4,3},{5,4},{6,5},{7,6},{8,15},{9,8},{10,9... | collective-permute-start | bytes 1769480 | tf_op jit(solution)/shard_map/ppermute | solution.py:280
  103.7 17.0 %collective-permute-start.7 = (bf16[2,128,1152]{2,1,0:T(8,128)(2,1)}, bf16[2,128,1152]{2,1,0:T(8,128)(2,1)}, u32[]{:S(2)}, u32[]{:S(2)}) collective-permute-start(bf16[2,128,1152]{2,1,0:T(8,128)(2,1)} %get-tuple-element.69), channel_id=1, source_target_pairs={{0,1},{1,2},{2,3},{3,4},{4,5},{5,6},{6,7},{7,0},{8,9},{9,10},{10,1... | collective-permute-start | bytes 1769480 | tf_op jit(solution)/shard_map/ppermute | solution.py:280
  103.7 17.0 %collective-permute-start.8 = (bf16[2,128,1152]{2,1,0:T(8,128)(2,1)}, bf16[2,128,1152]{2,1,0:T(8,128)(2,1)}, u32[]{:S(2)}, u32[]{:S(2)}) collective-permute-start(bf16[2,128,1152]{2,1,0:T(8,128)(2,1)} %get-tuple-element.70), channel_id=1, source_target_pairs={{0,7},{1,0},{2,1},{3,2},{4,3},{5,4},{6,5},{7,6},{8,15},{9,8},{10,9... | collective-permute-start | bytes 1769480 | tf_op jit(solution)/shard_map/ppermute | solution.py:280
  106.4 66.2 %all-to-all-start.1 = ((bf16[16,32,2176]{2,1,0:T(8,128)(2,1)}), bf16[16,32,2176]{2,1,0:T(8,128)(2,1)}, u32[]{:S(2)}, u32[]{:S(2)}) async-start(bf16[16,32,2176]{2,1,0:T(8,128)(2,1)} %bitcast.66), calls=%async_computation.1 | async-start | bytes 4456448 | tf_op jit(solution)/shard_map/all_to_all | solution.py:440
  117.5 16.8 %collective-permute-start.5 = (bf16[2,128,1152]{2,1,0:T(8,128)(2,1)}, bf16[2,128,1152]{2,1,0:T(8,128)(2,1)S(1)}, u32[]{:S(2)}, u32[]{:S(2)}) collective-permute-start(bf16[2,128,1152]{2,1,0:T(8,128)(2,1)} %get-tuple-element.67), channel_id=1, source_target_pairs={{0,1},{1,2},{2,3},{3,4},{4,5},{5,6},{6,7},{7,0},{8,9},{9,10},{10,1... | collective-permute-start | bytes 1769480 | tf_op jit(solution)/shard_map/ppermute | solution.py:280
  117.5 16.8 %collective-permute-start.6 = (bf16[2,128,1152]{2,1,0:T(8,128)(2,1)}, bf16[2,128,1152]{2,1,0:T(8,128)(2,1)S(1)}, u32[]{:S(2)}, u32[]{:S(2)}) collective-permute-start(bf16[2,128,1152]{2,1,0:T(8,128)(2,1)} %get-tuple-element.68), channel_id=1, source_target_pairs={{0,7},{1,0},{2,1},{3,2},{4,3},{5,4},{6,5},{7,6},{8,15},{9,8},{10,9... | collective-permute-start | bytes 1769480 | tf_op jit(solution)/shard_map/ppermute | solution.py:280
  124.4 22.5 %collective-permute-start.9 = (bf16[2,128,1152]{2,1,0:T(8,128)(2,1)}, bf16[2,128,1152]{2,1,0:T(8,128)(2,1)S(1)}, u32[]{:S(2)}, u32[]{:S(2)}) collective-permute-start(bf16[2,128,1152]{2,1,0:T(8,128)(2,1)} %get-tuple-element.75), channel_id=1, source_target_pairs={{0,1},{1,2},{2,3},{3,4},{4,5},{5,6},{6,7},{7,0},{8,9},{9,10},{10,1... | collective-permute-start | bytes 1769480 | tf_op jit(solution)/shard_map/ppermute | solution.py:280
  124.5 22.5 %collective-permute-start.10 = (bf16[2,128,1152]{2,1,0:T(8,128)(2,1)}, bf16[2,128,1152]{2,1,0:T(8,128)(2,1)S(1)}, u32[]{:S(2)}, u32[]{:S(2)}) collective-permute-start(bf16[2,128,1152]{2,1,0:T(8,128)(2,1)} %get-tuple-element.76), channel_id=1, source_target_pairs={{0,7},{1,0},{2,1},{3,2},{4,3},{5,4},{6,5},{7,6},{8,15},{9,8},{10,9... | collective-permute-start | bytes 1769480 | tf_op jit(solution)/shard_map/ppermute | solution.py:280
  137.8 18.0 %collective-permute-start.12 = (bf16[2,128,1152]{2,1,0:T(8,128)(2,1)}, bf16[2,128,1152]{2,1,0:T(8,128)(2,1)S(1)}, u32[]{:S(2)}, u32[]{:S(2)}) collective-permute-start(bf16[2,128,1152]{2,1,0:T(8,128)(2,1)} %get-tuple-element.81), channel_id=1, source_target_pairs={{0,8},{1,9},{2,10},{3,11},{4,12},{5,13},{6,14},{7,15},{8,0},{9,1},... | collective-permute-start | bytes 1769480 | tf_op jit(solution)/shard_map/ppermute | solution.py:284
  140.3 1.0 copy-start.1
  150.5 18.1 %collective-permute-start.11 = (bf16[2,128,1152]{2,1,0:T(8,128)(2,1)}, bf16[2,128,1152]{2,1,0:T(8,128)(2,1)S(1)}, u32[]{:S(2)}, u32[]{:S(2)}) collective-permute-start(bf16[2,128,1152]{2,1,0:T(8,128)(2,1)} %get-tuple-element.79), channel_id=1, source_target_pairs={{0,8},{1,9},{2,10},{3,11},{4,12},{5,13},{6,14},{7,15},{8,0},{9,1},... | collective-permute-start | bytes 1769480 | tf_op jit(solution)/shard_map/ppermute | solution.py:284
  157.3 18.3 %collective-permute-start.15 = (bf16[1,128,1152]{2,1,0:T(8,128)(2,1)}, bf16[1,128,1152]{2,1,0:T(8,128)(2,1)S(1)}, u32[]{:S(2)}, u32[]{:S(2)}) collective-permute-start(bf16[1,128,1152]{2,1,0:T(8,128)(2,1)} %get-tuple-element.86), channel_id=1, source_target_pairs={{0,1},{1,2},{2,3},{3,4},{4,5},{5,6},{6,7},{7,0},{8,9},{9,10},{10,1... | collective-permute-start | bytes 884744 | tf_op jit(solution)/shard_map/ppermute | solution.py:280
  157.3 18.3 %collective-permute-start.16 = (bf16[1,128,1152]{2,1,0:T(8,128)(2,1)}, bf16[1,128,1152]{2,1,0:T(8,128)(2,1)S(1)}, u32[]{:S(2)}, u32[]{:S(2)}) collective-permute-start(bf16[1,128,1152]{2,1,0:T(8,128)(2,1)} %get-tuple-element.87), channel_id=1, source_target_pairs={{0,7},{1,0},{2,1},{3,2},{4,3},{5,4},{6,5},{7,6},{8,15},{9,8},{10,9... | collective-permute-start | bytes 884744 | tf_op jit(solution)/shard_map/ppermute | solution.py:280
  168.5 4.1 %copy-start.4 = (bf16[128,2]{0,1:T(2,128)(2,1)S(1)}, bf16[128,2]{0,1:T(2,128)(2,1)}, u32[]{:S(2)}) copy-start(bf16[128,2]{0,1:T(2,128)(2,1)} %param.9) | copy-start | bytes 1540
  168.5 4.1 %copy-start.5 = (s32[2,128]{1,0:T(2,128)S(1)}, s32[2,128]{1,0:T(2,128)}, u32[]{:S(2)}) copy-start(s32[2,128]{1,0:T(2,128)} %get-tuple-element.47.target_ref) | copy-start | bytes 3076
  170.0 8.4 %copy-start.2 = (f32[2,128,1152]{2,1,0:T(8,128)S(1)}, f32[2,128,1152]{2,1,0:T(8,128)}, u32[]{:S(2)}) copy-start(f32[2,128,1152]{2,1,0:T(8,128)} %copy-done.1) | copy-start | bytes 3538948
  170.0 8.4 %collective-permute-start.13 = (bf16[1,128,1152]{2,1,0:T(8,128)(2,1)}, bf16[1,128,1152]{2,1,0:T(8,128)(2,1)S(1)}, u32[]{:S(2)}, u32[]{:S(2)}) collective-permute-start(bf16[1,128,1152]{2,1,0:T(8,128)(2,1)} %get-tuple-element.84), channel_id=1, source_target_pairs={{0,1},{1,2},{2,3},{3,4},{4,5},{5,6},{6,7},{7,0},{8,9},{9,10},{10,1... | collective-permute-start | bytes 884744 | tf_op jit(solution)/shard_map/ppermute | solution.py:280
  170.0 8.4 %collective-permute-start.14 = (bf16[1,128,1152]{2,1,0:T(8,128)(2,1)}, bf16[1,128,1152]{2,1,0:T(8,128)(2,1)S(1)}, u32[]{:S(2)}, u32[]{:S(2)}) collective-permute-start(bf16[1,128,1152]{2,1,0:T(8,128)(2,1)} %get-tuple-element.85), channel_id=1, source_target_pairs={{0,7},{1,0},{2,1},{3,2},{4,3},{5,4},{6,5},{7,6},{8,15},{9,8},{10,9... | collective-permute-start | bytes 884744 | tf_op jit(solution)/shard_map/ppermute | solution.py:280
